TPU v7x, 128 devices: a whole 4x4x4 slice. The times are simulated.
128 devices in a mesh: gx: 8 (over z, core), gy: 16 (over y, x).
Axes of the slice: x: 4, y: 4, z: 4, core: 2. Of those that a mesh axis runs over, the one named last changes fastest.
Arguments:
- positions: float32 [3, 64, 128, 256], P(None, 'gx', 'gy'), may hold values from 0 to 1
- charges: float32 [64, 128, 256], P('gx', 'gy'), may hold values from -0.3 to 0.3
- counts: int32 [64, 128, 8], P('gx', 'gy'), may hold values from 8 to 32, as said below
- compress: float32 [512, 128], replicated, may hold values from -0.25 to 0.25
- operators: float32 [316, 128, 128], replicated, may hold values from -0.1875 to 0.1875
- expand: float32 [128, 512], replicated, may hold values from -2 to 2
Outputs:
- potential: float32 [64, 128, 256], P('gx', 'gy')
Inputs may be any that keep to these rules, and one draw needn't show every extreme that they name: `counts`: some leaf holds exactly 32 particles in every draw.
All inputs are finite; a program needn't handle non-finite values.
Results may differ from a plain program's by a relative error of at most 0.00011.
Values sent between devices are 32-bit elements; how exact they have to be, the bound alone decides.
No kernel may reach another device: no remote copies, remote signals or barrier semaphores. Data moves between devices by JAX's collectives and lax.ppermute only.
A program may use at most 448 MiB of HBM per device.

v0:
```python
import jax
import jax.numpy as jnp
from jax import lax
from jax.sharding import PartitionSpec as P

ORDER = 8
COEF = 512
BLOCK = 8
SLOTS = 32


PRECISE = lax.Precision.HIGHEST
SOFTENING = 0.01


def extended_2(block, sides, width):
    for axis, dim in sides:
        count = lax.axis_size(axis)
        forward = [(i, i + 1) for i in range(count - 1)]
        backward = [(target, source) for source, target in forward]
        low = lax.ppermute(
            lax.slice_in_dim(block, block.shape[dim] - width, None, axis=dim), axis, forward
        )
        high = lax.ppermute(lax.slice_in_dim(block, 0, width, axis=dim), axis, backward)
        block = jnp.concatenate([low, block, high], axis=dim)
    return block


def cheb_weights(points, degree):
    angles = jnp.pi * (2.0 * jnp.arange(degree, dtype=jnp.float32) + 1.0) / (2.0 * degree)
    harmonic = jnp.arange(1, degree, dtype=jnp.float32)
    phases = jnp.arccos(jnp.clip(points, -1.0, 1.0))
    series = jnp.cos(harmonic[:, None] * phases[None, :])
    node_series = jnp.cos(harmonic[:, None] * angles[None, :])
    return 1.0 / degree + 2.0 / degree * jnp.dot(node_series.T, series, precision=PRECISE)


def transfer_matrix(degree):
    angles = jnp.pi * (2.0 * jnp.arange(degree, dtype=jnp.float32) + 1.0) / (2.0 * degree)
    node_points = jnp.cos(angles)
    child_sides = jnp.array([-1.0, 1.0], dtype=jnp.float32)
    shifted = 0.5 * (node_points[None, :] + child_sides[:, None])
    factor = cheb_weights(shifted.reshape(-1), degree).reshape(degree, 2, degree).transpose(1, 2, 0)
    product = (
        factor[:, None, None, :, None, None, :, None, None]
        * factor[None, :, None, None, :, None, None, :, None]
        * factor[None, None, :, None, None, :, None, None, :]
    )
    return product.reshape(8 * degree**3, degree**3)


def upward(children, transfer):
    side_x, side_y, side_z, columns = children.shape
    grouped = children.reshape(side_x // 2, 2, side_y // 2, 2, side_z // 2, 2, columns).transpose(
        0, 2, 4, 1, 3, 5, 6
    )
    flattened = grouped.reshape(side_x // 2 * (side_y // 2) * (side_z // 2), 8 * columns)
    return jnp.dot(flattened, transfer, precision=PRECISE).reshape(
        side_x // 2, side_y // 2, side_z // 2, columns
    )


def downward(parent, transfer):
    side_x, side_y, side_z, columns = parent.shape
    flattened = jnp.dot(
        parent.reshape(side_x * side_y * side_z, columns), transfer.T, precision=PRECISE
    )
    grouped = flattened.reshape(side_x, side_y, side_z, 2, 2, 2, columns).transpose(
        0, 3, 1, 4, 2, 5, 6
    )
    return grouped.reshape(2 * side_x, 2 * side_y, 2 * side_z, columns)


def full_operators(operators):
    reduced = operators.shape[-1]
    pieces = []
    cursor = 0
    for offset_x in range(7):
        for offset_y in range(7):
            if abs(offset_x - 3) <= 1 and abs(offset_y - 3) <= 1:
                pieces.append(operators[cursor : cursor + 2])
                pieces.append(jnp.zeros((3, reduced, reduced), operators.dtype))
                pieces.append(operators[cursor + 2 : cursor + 4])
                cursor += 4
            else:
                pieces.append(operators[cursor : cursor + 7])
                cursor += 7
    return jnp.concatenate(pieces, 0).reshape(7, 7, 7, reduced, reduced)


def windows(padded, count_x, count_y, count_z):
    reduced = padded.shape[-1]
    paired = padded.reshape(count_x + 2, 2, count_y + 2, 2, count_z + 2, 2, reduced)
    along_x = jnp.stack([paired[lag_index : lag_index + count_x] for lag_index in range(3)], axis=1)
    along_y = jnp.stack(
        [along_x[:, :, :, lag_index : lag_index + count_y] for lag_index in range(3)], axis=4
    )
    along_z = jnp.stack(
        [along_y[:, :, :, :, :, :, lag_index : lag_index + count_z] for lag_index in range(3)],
        axis=7,
    )
    ordered = along_z.transpose(0, 3, 6, 1, 2, 4, 5, 7, 8, 9)
    return ordered.reshape(count_x * count_y * count_z, 216 * reduced)


def translate(sources, operator_grid):
    reduced = operator_grid.shape[-1]
    outputs = []
    for parity in range(8):
        parity_x = parity // 4
        parity_y = parity // 2 % 2
        parity_z = parity % 2
        operator_block = operator_grid[
            1 - parity_x : 7 - parity_x, 1 - parity_y : 7 - parity_y, 1 - parity_z : 7 - parity_z
        ]
        outputs.append(
            jnp.dot(sources, operator_block.reshape(216 * reduced, reduced), precision=PRECISE)
        )
    return jnp.stack(outputs, 0)


def spread_children(children_parts, count_x, count_y, count_z):
    reduced = children_parts.shape[-1]
    grouped = children_parts.reshape(2, 2, 2, count_x, count_y, count_z, reduced).transpose(
        3, 0, 4, 1, 5, 2, 6
    )
    return grouped.reshape(2 * count_x, 2 * count_y, 2 * count_z, reduced)


def particle_basis(points, slot_count):
    unrolled = 2.0 * points.reshape(3, -1) - 1.0
    return [
        cheb_weights(unrolled[component], ORDER).reshape(ORDER, -1, slot_count)
        for component in range(3)
    ]


def leaf_multipoles(points, weighted, slot_count):
    basis_x, basis_y, basis_z = particle_basis(points, slot_count)
    masses = weighted.reshape(-1, slot_count)
    moments = jnp.einsum(
        "ls,als,bls,gls->labg", masses, basis_x, basis_y, basis_z, precision=PRECISE
    )
    return moments.reshape(masses.shape[0], ORDER**3)


def far_field(points, expansions, slot_count):
    basis_x, basis_y, basis_z = particle_basis(points, slot_count)
    shaped = expansions.reshape(-1, ORDER, ORDER, ORDER)
    return jnp.einsum("labg,als,bls,gls->ls", shaped, basis_x, basis_y, basis_z, precision=PRECISE)


def near_field(padded, count_x, count_y, count_z):
    slot_count = padded.shape[-1]
    centre = padded[:, 1 : 1 + count_x, 1 : 1 + count_y, 1 : 1 + count_z]
    others = 1.0 - jnp.eye(slot_count, dtype=padded.dtype)
    summed = jnp.zeros(centre.shape[1:], padded.dtype)
    for shift_x in (-1, 0, 1):
        for shift_y in (-1, 0, 1):
            for shift_z in (-1, 0, 1):
                source = padded[
                    :,
                    1 + shift_x : 1 + shift_x + count_x,
                    1 + shift_y : 1 + shift_y + count_y,
                    1 + shift_z : 1 + shift_z + count_z,
                ]
                squared = None
                for component, offset in ((0, shift_x), (1, shift_y), (2, shift_z)):
                    spacing = (
                        centre[component][..., :, None] - source[component][..., None, :] - offset
                    )
                    squared = spacing * spacing if squared is None else squared + spacing * spacing
                kernel = source[3][..., None, :] * lax.rsqrt(squared + SOFTENING)
                if shift_x == 0 and shift_y == 0 and (shift_z == 0):
                    kernel = kernel * others
                summed = summed + jnp.sum(kernel, axis=-1)
    return summed


def reduce_grid(grid_values, compress):
    shape_head = grid_values.shape[:3]
    return jnp.dot(grid_values.reshape(-1, COEF), compress, precision=PRECISE).reshape(
        shape_head + (compress.shape[1],)
    )


def expand_grid(grid_values, expand):
    shape_head = grid_values.shape[:3]
    return jnp.dot(grid_values.reshape(-1, expand.shape[0]), expand, precision=PRECISE).reshape(
        shape_head + (COEF,)
    )


def pad_depth(extended):
    return jnp.pad(extended, ((0, 0), (0, 0), (2, 2), (0, 0)))


def per_device(positions, charges, counts, compress, operators, expand):
    slot_count = SLOTS
    leaf_side = BLOCK
    parent_side = leaf_side // 2
    grand_side = leaf_side // 4
    occupied = jnp.arange(slot_count, dtype=jnp.int32)[None, None, None, :] < counts[..., None]
    occupied = occupied.astype(jnp.float32).reshape(leaf_side, leaf_side, leaf_side * slot_count)
    weighted = charges * occupied
    transfer = transfer_matrix(ORDER)
    leaf_m = leaf_multipoles(positions, weighted, slot_count).reshape(
        leaf_side, leaf_side, leaf_side, COEF
    )
    parent_m = upward(leaf_m, transfer)
    grand_m = upward(parent_m, transfer)
    leaf_c = reduce_grid(leaf_m, compress)
    parent_c = reduce_grid(parent_m, compress)
    grand_c = reduce_grid(grand_m, compress)
    leaf_ext = pad_depth(extended_2(leaf_c, (("gx", 0), ("gy", 1)), 2))
    parent_ext = pad_depth(extended_2(parent_c, (("gx", 0), ("gy", 1)), 2))
    grand_ext = pad_depth(extended_2(grand_c, (("gx", 0), ("gy", 1)), 2))
    stacked = jnp.concatenate([positions, weighted[None]], 0)
    ghosts = extended_2(stacked, (("gx", 1), ("gy", 2)), 1)
    ghosts = ghosts.reshape(4, leaf_side + 2, leaf_side + 2, leaf_side, slot_count)
    ghosts = jnp.pad(ghosts, ((0, 0), (0, 0), (0, 0), (1, 1), (0, 0)))
    near_part = near_field(ghosts, leaf_side, leaf_side, leaf_side)
    top_side = grand_side // 2
    sources = jnp.concatenate(
        [
            windows(leaf_ext, parent_side, parent_side, parent_side),
            windows(parent_ext, grand_side, grand_side, grand_side),
            windows(grand_ext, top_side, top_side, top_side),
        ],
        0,
    )
    operator_grid = full_operators(operators)
    translated = translate(sources, operator_grid)
    leaf_rows = parent_side**3
    middle_rows = grand_side**3
    leaf_lc = (
        spread_children(translated[:, :leaf_rows], parent_side, parent_side, parent_side) * 1.0
    )
    parent_lc = (
        spread_children(
            translated[:, leaf_rows : leaf_rows + middle_rows], grand_side, grand_side, grand_side
        )
        * 0.5
    )
    grand_lc = (
        spread_children(translated[:, leaf_rows + middle_rows :], top_side, top_side, top_side)
        * 0.25
    )
    grand_l = expand_grid(grand_lc, expand)
    parent_l = expand_grid(parent_lc, expand) + downward(grand_l, transfer)
    leaf_l = expand_grid(leaf_lc, expand) + downward(parent_l, transfer)
    far_part = far_field(positions, leaf_l.reshape(-1, COEF), slot_count)
    far_part = far_part.reshape(leaf_side, leaf_side, leaf_side * slot_count)
    near_part = near_part.reshape(leaf_side, leaf_side, leaf_side * slot_count)
    return (far_part + near_part) * occupied


def solution(mesh):
    placed = (P(None, "gx", "gy", None), P("gx", "gy", None), P("gx", "gy", None), P(), P(), P())
    return jax.shard_map(
        per_device, mesh=mesh, in_specs=placed, out_specs=P("gx", "gy", None), check_vma=False
    )
```

profile of v0, /device:TPU:41, one launch (start us, length us, event | category | flops | bytes accessed | tf_op | source)
XLA Modules:
  0.0 950.0 jit_solution(12113821101177518055)
XLA Ops:
  27.1 18.9 %fusion.9 = f32[512,8,8,8]{1,2,3,0:T(8,128)} fusion(f32[512,32,8]{1,2,0:T(8,128)S(1)} %copy.87, f32[512,32,8]{1,2,0:T(8,128)S(1)} %copy-done.6, f32[8,512,32,1]{2,1,0,3:T(8,128)S(1)} %multiply_bitcast_fusion), kind=kOutput, calls=%fused_computation.86 | convolution fusion | flops 101711872 | bytes 2621440 | tf_op jit(solution)/shard_map/ls,als,bls,gls->labg/dot_general | solution.py:141
  46.0 18.1 %copy.97 = f32[512,8,8,8]{3,2,1,0:T(8,128)} copy(f32[512,8,8,8]{1,2,3,0:T(8,128)} %fusion.9) | data formatting | bytes 2097152 | tf_op jit(solution)/shard_map/ls,als,bls,gls->labg/transpose | solution.py:141
  64.1 12.2 %reshape_reshape_reshape.7 = f32[4,2,4,2,4,2,512]{6,5,4,3,2,1,0:T(2,128)S(1)} reshape(f32[512,8,8,8]{3,2,1,0:T(8,128)} %copy.97) | data formatting | bytes 2097152 | tf_op jit(solution)/shard_map/reshape;reshape;reshape | solution.py:54
  78.7 41.6 %broadcast_multiply_fusion = f32[2,2,2,8,8,8,8,8,8]{8,7,6,5,4,3,2,1,0:T(8,128)} fusion(f32[2,8,8]{2,1,0:T(8,128)S(1)} %copy.99, f32[2,2,8,8,8,8]{5,4,3,2,1,0:T(8,128)S(1)} %broadcast_multiply_fusion.1), kind=kLoop, calls=%fused_computation | loop fusion | flops 2097152 | bytes 8454656 | tf_op jit(solution)/shard_map/mul | solution.py:45
  120.3 94.7 %mul.867 = f32[4096,512]{1,0:T(8,128)} reshape(f32[2,2,2,8,8,8,8,8,8]{8,7,6,5,4,3,2,1,0:T(8,128)} %broadcast_multiply_fusion) | data formatting | bytes 16777216 | tf_op jit(solution)/shard_map/mul | solution.py:45
  240.4 11.0 %copy.92 = f32[512,8,8,8]{0,3,2,1:T(8,128)S(1)} copy(f32[512,8,8,8]{1,2,3,0:T(8,128)} %fusion.9) | data formatting | bytes 2097152 | tf_op jit(solution)/shard_map/ls,als,bls,gls->labg/transpose | solution.py:141
  296.0 71.3 %fusion.152 = (f32[6,6,6,128,128]{4,3,2,1,0:T(8,128)}, f32[6,6,6,128,128]{4,3,2,1,0:T(8,128)}, f32[6,6,6,128,128]{4,3,2,1,0:T(8,128)}, f32[6,6,6,128,128]{4,3,2,...) fusion(f32[7,7,7,128,128]{4,3,2,1,0:T(8,128)} %bitcast.53), kind=kLoop, calls=%fused_computation.396 | loop fusion | bytes 226492416 | tf_op jit(solution)/shard_map/slice | solution.py:113
  371.4 10.1 %fusion.191 = f32[8,512,32,8]{2,0,3,1:T(8,128)} fusion(f32[512,32,8]{1,2,0:T(8,128)} %copy.88, f32[512,32,8]{1,2,0:T(8,128)S(1)} %copy-done.3), kind=kLoop, calls=%fused_computation.82.clone.clone.clone.1 | loop fusion | flops 1048576 | bytes 5242880 | tf_op jit(solution)/shard_map/labg,als,bls,gls->ls/dot_general | solution.py:150
  385.4 21.3 %mul.876 = f32[2,2,8,8,8,8,8,8]{7,6,5,4,3,2,1,0:T(8,128)} broadcast(f32[2,2,8,8,8,8]{5,4,3,2,1,0:T(8,128)S(1)} %broadcast_multiply_fusion.1), dimensions={0,1,2,3,5,6} | broadcast | bytes 4259840 | tf_op jit(solution)/shard_map/mul | solution.py:45
  406.7 48.3 %mul.877 = f32[2,2,512,512]{3,2,1,0:T(8,128)} reshape(f32[2,2,8,8,8,8,8,8]{7,6,5,4,3,2,1,0:T(8,128)} %mul.876) | data formatting | bytes 8388608 | tf_op jit(solution)/shard_map/mul | solution.py:45
  455.0 11.2 %mul.879 = f32[2,8,8,8,8,8,8]{6,5,4,3,2,1,0:T(8,128)} broadcast(f32[2,8,8]{2,1,0:T(8,128)S(1)} %copy-done.42), dimensions={0,3,6} | broadcast | bytes 2097664 | tf_op jit(solution)/shard_map/mul | solution.py:45
  466.2 25.1 %mul.880 = f32[2,512,512]{2,1,0:T(8,128)} reshape(f32[2,8,8,8,8,8,8]{6,5,4,3,2,1,0:T(8,128)} %mul.879) | data formatting | bytes 4194304 | tf_op jit(solution)/shard_map/mul | solution.py:45
  542.7 21.0 %multiply_reduce_fusion.2 = (f32[8,8,8,32]{3,2,1,0:T(8,128)}, f32[8,8,8,32]{3,2,1,0:T(8,128)S(1)}, f32[8,8,8,32]{3,2,1,0:T(8,128)S(1)}) fusion(f32[8,8,8,32]{3,2,1,0:T(8,128)S(1)} %get-tuple-element.117, f32[8,8,8,32]{3,2,1,0:T(8,128)S(1)} %get-tuple-element.116, f32[8,8,8,32]{3,2,1,0:T(8,128)S(1)} %get-tuple-element.115, ...), kind=kLoop, calls=%fused_computation.95 | loop fusion | flops 21446656 | bytes 1179648 | tf_op jit(solution)/shard_map/reduce_sum | solution.py:176
  563.7 27.0 %multiply_reduce_fusion.13 = (f32[8,8,8,32]{3,2,1,0:T(8,128)S(1)}, f32[8,8,8,32]{3,2,1,0:T(8,128)S(1)}, f32[8,8,8,32]{3,2,1,0:T(8,128)}, f32[8,8,8,32]{3,2,1,0:T(8,128)}) fusion(f32[32,32]{1,0:T(8,128)S(1)} %copy-done.44, f32[8,8,8,32]{3,2,1,0:T(8,128)S(1)} %get-tuple-element.152, f32[8,8,8,32]{3,2,1,0:T(8,128)S(1)} %get-tuple-element.153, ...), kind=kLoop, calls=%fused_computation.106 | loop fusion | flops 26673152 | bytes 1314816 | tf_op jit(solution)/shard_map/reduce_sum | solution.py:176
  590.6 26.2 %multiply_reduce_fusion.15 = (f32[8,8,8,32]{3,2,1,0:T(8,128)S(1)}, f32[8,8,8,32]{3,2,1,0:T(8,128)S(1)}, f32[8,8,8,32]{3,2,1,0:T(8,128)S(1)}, f32[8,8,8,32]{3,2,1,0:T(8,128)S(1)}) fusion(f32[8,8,8,32]{3,2,1,0:T(8,128)} %get-tuple-element.79, f32[8,8,8,32]{3,2,1,0:T(8,128)} %get-tuple-element.78, f32[8,8,8,32]{3,2,1,0:T(8,128)} %get-tuple-element.77, ...), kind=kLoop, calls=%fused_computation.108 | loop fusion | flops 26148864 | bytes 1507328 | tf_op jit(solution)/shard_map/reduce_sum | solution.py:176
  616.9 27.1 %multiply_reduce_fusion.9 = (f32[8,8,8,32]{3,2,1,0:T(8,128)}, f32[8,8,8,32]{3,2,1,0:T(8,128)S(1)}, f32[8,8,8,32]{3,2,1,0:T(8,128)S(1)}, f32[8,8,8,32]{3,2,1,0:T(8,128)S(1)}) fusion(f32[8,8,8,32]{3,2,1,0:T(8,128)} %get-tuple-element.96, f32[8,8,8,32]{3,2,1,0:T(8,128)} %get-tuple-element.95, f32[8,8,8,32]{3,2,1,0:T(8,128)} %get-tuple-element.94, ...), kind=kLoop, calls=%fused_computation.102 | loop fusion | flops 27721728 | bytes 1507328 | tf_op jit(solution)/shard_map/reduce_sum | solution.py:176
  644.1 24.9 %multiply_reduce_fusion.26 = (f32[8,8,8,32]{3,2,1,0:T(8,128)S(1)}, f32[8,8,8,32]{3,2,1,0:T(8,128)S(1)}, f32[8,8,8,32]{3,2,1,0:T(8,128)S(1)}, f32[8,8,8,32]{3,2,1,0:T(8,128)S(1)}) fusion(f32[8,8,8,32]{3,2,1,0:T(8,128)S(1)} %get-tuple-element.51, f32[8,8,8,32]{3,2,1,0:T(8,128)S(1)} %get-tuple-element.152, f32[8,8,8,32]{3,2,1,0:T(8,128)S(1)} %get-tuple-element.50, ...), kind=kLoop, calls=%fused_computation.119 | loop fusion | flops 27721728 | bytes 1507328 | tf_op jit(solution)/shard_map/reduce_sum | solution.py:176
  669.1 25.3 %multiply_reduce_fusion.19 = (f32[8,8,8,32]{3,2,1,0:T(8,128)S(1)}, f32[8,8,8,32]{3,2,1,0:T(8,128)S(1)}, f32[8,8,8,32]{3,2,1,0:T(8,128)S(1)}, f32[8,8,8,32]{3,2,1,0:T(8,128)S(1)}) fusion(f32[8,8,8,32]{3,2,1,0:T(8,128)S(1)} %get-tuple-element.145, f32[8,8,8,32]{3,2,1,0:T(8,128)S(1)} %get-tuple-element.146, f32[8,8,8,32]{3,2,1,0:T(8,128)S(1)} %get-tuple-element.147, ...), kind=kLoop, calls=%fused_computation.112 | loop fusion | flops 27197440 | bytes 1507328 | tf_op jit(solution)/shard_map/reduce_sum | solution.py:176
  694.4 26.4 %multiply_reduce_fusion.6 = (f32[8,8,8,32]{3,2,1,0:T(8,128)}, f32[8,8,8,32]{3,2,1,0:T(8,128)}, f32[8,8,8,32]{3,2,1,0:T(8,128)}, f32[8,8,8,32]{3,2,1,0:T(8,128)}) fusion(f32[8,8,8,32]{3,2,1,0:T(8,128)S(1)} %copy-done.27, f32[8,8,8,32]{3,2,1,0:T(8,128)S(1)} %copy-done.26, f32[8,8,8,32]{3,2,1,0:T(8,128)S(1)} %copy-done.25, f32[8,8,8,32]{3,2,1,0:T(8,128)S(1)} %copy-done.24, ...), kind=kLoop, calls=%fused_computation.99 | loop fusion | flops 27197440 | bytes 1507328 | tf_op jit(solution)/shard_map/reduce_sum | solution.py:176
  749.7 13.1 %maximum_bitcast_fusion = f32[4,4,4,3,2,3,2,3,2,128]{9,4,0,8,2,6,1,3,5,7:T(2,128)} fusion(f32[4,3,2,4,3,2,4,1,2,128]{9,2,0,8,6,5,3,1,4,7:T(2,128)} %get-tuple-element.43, f32[4,3,2,4,3,2,4,1,2,128]{9,2,0,8,6,5,3,1,4,7:T(2,128)} %get-tuple-element.44, f32[4,3,2,4,3,2,4,1,2,128]{9,2,0,8,6,5,3,1,4,7:T(2,128)} %get-tuple-element.42), kind=kLoop, calls=%fused_computation.126 | loop fusion | flops 3538944 | bytes 14155776 | tf_op jit(solution)/shard_map/transpose | solution.py:102
  762.8 9.6 %copy.96 = f32[4,4,4,3,2,3,2,3,2,128]{9,8,7,6,5,4,3,2,1,0:T(2,128)} copy(f32[4,4,4,3,2,3,2,3,2,128]{9,4,0,8,2,6,1,3,5,7:T(2,128)} %maximum_bitcast_fusion) | data formatting | bytes 14155776 | tf_op jit(solution)/shard_map/transpose | solution.py:102
  781.6 13.6 %fusion.45 = f32[8,73,128]{2,1,0:T(8,128)S(1)} fusion(f32[27648,128]{1,0:T(8,128)} %bitcast.482, f32[1,27648]{1,0:T(1,128)S(1)} %bitcast.486, f32[8,27648]{1,0:T(8,128)S(1)} %reshape.405, f32[64,27648]{1,0:T(8,128)} %reshape.401), kind=kOutput, calls=%fused_computation.172 | convolution fusion | flops 3104151552 | bytes 22269952 | tf_op jit(solution)/shard_map/dot_general | solution.py:117
  795.2 12.7 %fusion.44 = f32[8,73,128]{2,1,0:T(8,128)S(1)} fusion(f32[8,73,128]{2,1,0:T(8,128)S(1)} %fusion.45, f32[27648,128]{1,0:T(8,128)} %bitcast.481, f32[1,27648]{1,0:T(1,128)S(1)} %bitcast.487, f32[8,27648]{1,0:T(8,128)S(1)} %reshape.405, f32[64,27648]{1,0:T(8,128)S(1)} %copy-done.1), kind=kOutput, calls=%fused_computation.170 | convolution fusion | flops 3104151552 | bytes 22269952 | tf_op jit(solution)/shard_map/dot_general | solution.py:117
  807.9 12.7 %fusion.43 = f32[8,73,128]{2,1,0:T(8,128)S(1)} fusion(f32[8,73,128]{2,1,0:T(8,128)S(1)} %fusion.44, f32[27648,128]{1,0:T(8,128)} %bitcast.480, f32[1,27648]{1,0:T(1,128)S(1)} %bitcast.488, f32[8,27648]{1,0:T(8,128)S(1)} %reshape.405, f32[64,27648]{1,0:T(8,128)S(1)} %copy-done.1), kind=kOutput, calls=%fused_computation.168 | convolution fusion | flops 3104151552 | bytes 22269952 | tf_op jit(solution)/shard_map/dot_general | solution.py:117
  820.6 12.9 %fusion.42 = f32[8,73,128]{2,1,0:T(8,128)S(1)} fusion(f32[8,73,128]{2,1,0:T(8,128)S(1)} %fusion.43, f32[27648,128]{1,0:T(8,128)} %bitcast.479, f32[1,27648]{1,0:T(1,128)S(1)} %bitcast.489, f32[8,27648]{1,0:T(8,128)S(1)} %reshape.405, f32[64,27648]{1,0:T(8,128)S(1)} %copy-done.1), kind=kOutput, calls=%fused_computation.166 | convolution fusion | flops 3104151552 | bytes 22269952 | tf_op jit(solution)/shard_map/dot_general | solution.py:117
  833.5 12.7 %fusion.41 = f32[8,73,128]{2,1,0:T(8,128)S(1)} fusion(f32[8,73,128]{2,1,0:T(8,128)S(1)} %fusion.42, f32[27648,128]{1,0:T(8,128)} %bitcast.478, f32[1,27648]{1,0:T(1,128)S(1)} %bitcast.490, f32[8,27648]{1,0:T(8,128)S(1)} %reshape.405, f32[64,27648]{1,0:T(8,128)S(1)} %copy-done.1), kind=kOutput, calls=%fused_computation.164 | convolution fusion | flops 3104151552 | bytes 22269952 | tf_op jit(solution)/shard_map/dot_general | solution.py:117
  846.2 12.7 %fusion.40 = f32[8,73,128]{2,1,0:T(8,128)S(1)} fusion(f32[8,73,128]{2,1,0:T(8,128)S(1)} %fusion.41, f32[27648,128]{1,0:T(8,128)} %bitcast.477, f32[1,27648]{1,0:T(1,128)S(1)} %bitcast.491, f32[8,27648]{1,0:T(8,128)S(1)} %reshape.405, f32[64,27648]{1,0:T(8,128)S(1)} %copy-done.1), kind=kOutput, calls=%fused_computation.162 | convolution fusion | flops 3104151552 | bytes 22269952 | tf_op jit(solution)/shard_map/dot_general | solution.py:117
  858.9 13.1 %fusion.39 = f32[8,73,128]{2,1,0:T(8,128)S(1)} fusion(f32[8,73,128]{2,1,0:T(8,128)S(1)} %fusion.40, f32[27648,128]{1,0:T(8,128)} %bitcast.476, f32[1,27648]{1,0:T(1,128)S(1)} %bitcast.492, f32[8,27648]{1,0:T(8,128)S(1)} %reshape.405, f32[64,27648]{1,0:T(8,128)S(1)} %copy-done.1), kind=kOutput, calls=%fused_computation.160 | convolution fusion | flops 3104151552 | bytes 22269952 | tf_op jit(solution)/shard_map/dot_general | solution.py:117
  872.0 13.0 %fusion.38 = f32[8,73,128]{2,1,0:T(8,128)S(1)} fusion(f32[8,73,128]{2,1,0:T(8,128)S(1)} %fusion.39, f32[27648,128]{1,0:T(8,128)} %bitcast.475, f32[1,27648]{1,0:T(1,128)S(1)} %bitcast.493, f32[8,27648]{1,0:T(8,128)S(1)} %reshape.405, f32[64,27648]{1,0:T(8,128)S(1)} %copy-done.1), kind=kOutput, calls=%fused_computation.158 | convolution fusion | flops 3104151552 | bytes 22269952 | tf_op jit(solution)/shard_map/dot_general | solution.py:117
  893.3 11.3 %fusion.30 = f32[4,2,4,2,4,2,512]{6,4,5,3,1,2,0:T(4,128)S(1)} fusion(f32[4,4,4,512,1,1,1]{3,2,6,5,4,1,0:T(4,128)S(1)} %fusion.37, f32[2,512,512]{2,1,0:T(8,128)S(1)} %copy-done.14, f32[2,2,512,512]{3,2,1,0:T(8,128)} %mul.877), kind=kOutput, calls=%fused_computation.144 | convolution fusion | flops 1612709888 | bytes 7471104 | tf_op jit(solution)/shard_map/dot_general | solution.py:65
  907.1 11.1 %reshape_reshape.8 = f32[512,8,8,8]{3,2,1,0:T(8,128)} reshape(f32[8,8,8,512]{3,2,1,0:T(8,128)S(1)} %convolution_add_fusion) | data formatting | bytes 2097152 | tf_op jit(solution)/shard_map/reshape;reshape | solution.py:149
  918.2 30.6 %fusion.26 = f32[512,32]{1,0:T(8,128)S(1)} fusion(f32[512,8,8,8]{3,2,1,0:T(8,128)} %reshape_reshape.8, f32[512,32,8]{1,0,2:T(8,128)S(1)} %bitcast.484, f32[8,512,32,8]{2,0,3,1:T(8,128)} %fusion.191), kind=kOutput, calls=%fused_computation.136 | convolution fusion | flops 100909056 | bytes 5832704 | tf_op jit(solution)/shard_map/labg,als,bls,gls->ls/dot_general | solution.py:150
  (267 shorter events, 207.5 us)
Async XLA Ops:
  0.0 885.1 %copy-start = (f32[128,512]{1,0:T(8,128)S(1)}, f32[128,512]{1,0:T(8,128)}, u32[]{:S(2)}) copy-start(f32[128,512]{1,0:T(8,128)} %param.12) | copy-start | bytes 786436
  9.1 504.5 %copy-start.15 = (f32[8,8,256]{2,1,0:T(8,128)}, f32[8,8,256]{2,1,0:T(8,128)S(1)}, u32[]{:S(2)}) copy-start(f32[8,8,256]{2,1,0:T(8,128)S(1)} %get-tuple-element.32) | copy-start | bytes 196612
  228.2 263.2 %collective-permute-start.8 = (f32[2,2,2,128]{3,0,2,1:T(2,128)S(1)}, f32[2,2,2,128]{3,0,2,1:T(2,128)S(1)}, u32[]{:S(2)}, u32[]{:S(2)}) collective-permute-start(f32[2,2,2,128]{3,0,2,1:T(2,128)S(1)} %copy.104), channel_id=1, source_target_pairs={{0,16},{16,32},{32,48},{48,64},{64,80},{80,96},{96,112},{1,17},{17... | collective-permute-start | bytes 12296 | tf_op jit(solution)/shard_map/ppermute | solution.py:21
  232.3 261.1 %collective-permute-start.9 = (f32[2,2,2,128]{3,0,2,1:T(2,128)S(1)}, f32[2,2,2,128]{3,0,2,1:T(2,128)S(1)}, u32[]{:S(2)}, u32[]{:S(2)}) collective-permute-start(f32[2,2,2,128]{3,0,2,1:T(2,128)S(1)} %copy.104), channel_id=1, source_target_pairs={{16,0},{32,16},{48,32},{64,48},{80,64},{96,80},{112,96},{17,1},{33... | collective-permute-start | bytes 12296 | tf_op jit(solution)/shard_map/ppermute | solution.py:24
  234.8 273.3 %collective-permute-start.12 = (f32[4,1,8,256]{3,2,1,0:T(8,128)}, f32[4,1,8,256]{3,2,1,0:T(8,128)S(1)}, u32[]{:S(2)}, u32[]{:S(2)}) collective-permute-start(f32[4,1,8,256]{3,2,1,0:T(8,128)} %get-tuple-element.169), channel_id=1, source_target_pairs={{0,16},{16,32},{32,48},{48,64},{64,80},{80,96},{96,112},{1,17},{17... | collective-permute-start | bytes 98312 | tf_op jit(solution)/shard_map/ppermute | solution.py:21
  238.5 275.2 %collective-permute-start.13 = (f32[4,1,8,256]{3,2,1,0:T(8,128)}, f32[4,1,8,256]{3,2,1,0:T(8,128)}, u32[]{:S(2)}, u32[]{:S(2)}) collective-permute-start(f32[4,1,8,256]{3,2,1,0:T(8,128)} %get-tuple-element.170), channel_id=1, source_target_pairs={{16,0},{32,16},{48,32},{64,48},{80,64},{96,80},{112,96},{17,1},{33... | collective-permute-start | bytes 98312 | tf_op jit(solution)/shard_map/ppermute | solution.py:24
  254.6 270.4 %collective-permute-start = (f32[2,8,8,128]{3,0,2,1:T(2,128)}, f32[2,8,8,128]{3,0,2,1:T(2,128)}, u32[]{:S(2)}, u32[]{:S(2)}) collective-permute-start(f32[2,8,8,128]{3,0,2,1:T(2,128)} %copy.93), channel_id=1, source_target_pairs={{0,16},{16,32},{32,48},{48,64},{64,80},{80,96},{96,112},{1,17},{17... | collective-permute-start | bytes 196616 | tf_op jit(solution)/shard_map/ppermute | solution.py:21
  296.0 75.4 %copy-start.3 = (f32[512,32,8]{1,2,0:T(8,128)S(1)}, f32[512,32,8]{1,2,0:T(8,128)}, u32[]{:S(2)}) copy-start(f32[512,32,8]{1,2,0:T(8,128)} %copy-done.2) | copy-start | bytes 1572868
  406.7 48.3 %copy-start.42 = (f32[2,8,8]{2,1,0:T(8,128)S(1)}, f32[2,8,8]{2,1,0:T(8,128)}, u32[]{:S(2)}) copy-start(f32[2,8,8]{2,1,0:T(8,128)} %copy-done.41) | copy-start | bytes 1540
  491.3 4.5 collective-permute-start.4
  493.4 5.6 collective-permute-start.5
  495.9 7.5 collective-permute-start.10
  499.0 6.8 collective-permute-start.11
  503.3 21.7 %collective-permute-start.1 = (f32[2,8,8,128]{3,0,2,1:T(2,128)}, f32[2,8,8,128]{3,0,2,1:T(2,128)S(1)}, u32[]{:S(2)}, u32[]{:S(2)}) collective-permute-start(f32[2,8,8,128]{3,0,2,1:T(2,128)} %copy.94), channel_id=1, source_target_pairs={{16,0},{32,16},{48,32},{64,48},{80,64},{96,80},{112,96},{17,1},{33... | collective-permute-start | bytes 196616 | tf_op jit(solution)/shard_map/ppermute | solution.py:24
  505.8 10.8 %collective-permute-start.6 = (f32[8,2,4,128]{3,2,1,0:T(4,128)S(1)}, f32[8,2,4,128]{3,2,1,0:T(4,128)S(1)}, u32[]{:S(2)}, u32[]{:S(2)}) collective-permute-start(f32[8,2,4,128]{3,2,1,0:T(4,128)S(1)} %get-tuple-element.188), channel_id=1, source_target_pairs={{0,1},{1,2},{2,3},{3,4},{4,5},{5,6},{6,7},{7,8},{8,9},{9,10},{10,1... | collective-permute-start | bytes 98312 | tf_op jit(solution)/shard_map/ppermute | solution.py:21
  508.2 14.0 %collective-permute-start.7 = (f32[8,2,4,128]{3,2,1,0:T(4,128)S(1)}, f32[8,2,4,128]{3,2,1,0:T(4,128)S(1)}, u32[]{:S(2)}, u32[]{:S(2)}) collective-permute-start(f32[8,2,4,128]{3,2,1,0:T(4,128)S(1)} %get-tuple-element.189), channel_id=1, source_target_pairs={{1,0},{2,1},{3,2},{4,3},{5,4},{6,5},{7,6},{8,7},{9,8},{10,9},{11,1... | collective-permute-start | bytes 98312 | tf_op jit(solution)/shard_map/ppermute | solution.py:24
  514.6 19.6 %collective-permute-start.14 = (f32[4,10,1,256]{3,2,1,0:T(1,128)S(1)}, f32[4,10,1,256]{3,2,1,0:T(1,128)S(1)}, u32[]{:S(2)}, u32[]{:S(2)}) collective-permute-start(f32[4,10,1,256]{3,2,1,0:T(1,128)S(1)} %get-tuple-element.167), channel_id=1, source_target_pairs={{0,1},{1,2},{2,3},{3,4},{4,5},{5,6},{6,7},{7,8},{8,9},{9,10},{10,1... | collective-permute-start | bytes 122888 | tf_op jit(solution)/shard_map/ppermute | solution.py:21
  516.6 18.2 %collective-permute-start.15 = (f32[4,10,1,256]{3,2,1,0:T(1,128)S(1)}, f32[4,10,1,256]{3,2,1,0:T(1,128)}, u32[]{:S(2)}, u32[]{:S(2)}) collective-permute-start(f32[4,10,1,256]{3,2,1,0:T(1,128)S(1)} %get-tuple-element.168), channel_id=1, source_target_pairs={{1,0},{2,1},{3,2},{4,3},{5,4},{6,5},{7,6},{8,7},{9,8},{10,9},{11,1... | collective-permute-start | bytes 122888 | tf_op jit(solution)/shard_map/ppermute | solution.py:24
  526.6 210.9 %collective-permute-start.2 = (f32[12,2,8,128]{3,0,2,1:T(8,128)}, f32[12,2,8,128]{3,0,2,1:T(8,128)}, u32[]{:S(2)}, u32[]{:S(2)}) collective-permute-start(f32[12,2,8,128]{3,0,2,1:T(8,128)} %get-tuple-element.162), channel_id=1, source_target_pairs={{0,1},{1,2},{2,3},{3,4},{4,5},{5,6},{6,7},{7,8},{8,9},{9,10},{10,1... | collective-permute-start | bytes 294920 | tf_op jit(solution)/shard_map/ppermute | solution.py:21
  528.5 209.0 %collective-permute-start.3 = (f32[12,2,8,128]{3,0,2,1:T(8,128)}, f32[12,2,8,128]{3,0,2,1:T(8,128)}, u32[]{:S(2)}, u32[]{:S(2)}) collective-permute-start(f32[12,2,8,128]{3,0,2,1:T(8,128)} %get-tuple-element.163), channel_id=1, source_target_pairs={{1,0},{2,1},{3,2},{4,3},{5,4},{6,5},{7,6},{8,7},{9,8},{10,9},{11,1... | collective-permute-start | bytes 294920 | tf_op jit(solution)/shard_map/ppermute | solution.py:24
  563.7 53.2 %copy-start.28 = (f32[8,8,8,32]{3,2,1,0:T(8,128)S(1)}, f32[8,8,8,32]{3,2,1,0:T(8,128)}, u32[]{:S(2)}) copy-start(f32[8,8,8,32]{3,2,1,0:T(8,128)} %get-tuple-element.67) | copy-start | bytes 196612
  563.7 53.2 %copy-start.29 = (f32[8,8,8,32]{3,2,1,0:T(8,128)S(1)}, f32[8,8,8,32]{3,2,1,0:T(8,128)}, u32[]{:S(2)}) copy-start(f32[8,8,8,32]{3,2,1,0:T(8,128)} %get-tuple-element.86) | copy-start | bytes 196612
  590.6 78.4 %copy-start.18 = (f32[8,8,8,32]{3,2,1,0:T(8,128)S(1)}, f32[8,8,8,32]{3,2,1,0:T(8,128)}, u32[]{:S(2)}) copy-start(f32[8,8,8,32]{3,2,1,0:T(8,128)} %get-tuple-element.70) | copy-start | bytes 196612
  590.6 78.4 %copy-start.19 = (f32[8,8,8,32]{3,2,1,0:T(8,128)S(1)}, f32[8,8,8,32]{3,2,1,0:T(8,128)}, u32[]{:S(2)}) copy-start(f32[8,8,8,32]{3,2,1,0:T(8,128)} %get-tuple-element.71) | copy-start | bytes 196612
  590.6 78.4 %copy-start.20 = (f32[8,8,8,32]{3,2,1,0:T(8,128)S(1)}, f32[8,8,8,32]{3,2,1,0:T(8,128)}, u32[]{:S(2)}) copy-start(f32[8,8,8,32]{3,2,1,0:T(8,128)} %get-tuple-element.72) | copy-start | bytes 196612
  590.6 78.4 %copy-start.21 = (f32[8,8,8,32]{3,2,1,0:T(8,128)S(1)}, f32[8,8,8,32]{3,2,1,0:T(8,128)}, u32[]{:S(2)}) copy-start(f32[8,8,8,32]{3,2,1,0:T(8,128)} %get-tuple-element.73) | copy-start | bytes 196612
  590.6 78.4 %copy-start.22 = (f32[8,8,8,32]{3,2,1,0:T(8,128)S(1)}, f32[8,8,8,32]{3,2,1,0:T(8,128)}, u32[]{:S(2)}) copy-start(f32[8,8,8,32]{3,2,1,0:T(8,128)} %get-tuple-element.74) | copy-start | bytes 196612
  590.6 78.4 %copy-start.23 = (f32[8,8,8,32]{3,2,1,0:T(8,128)S(1)}, f32[8,8,8,32]{3,2,1,0:T(8,128)}, u32[]{:S(2)}) copy-start(f32[8,8,8,32]{3,2,1,0:T(8,128)} %get-tuple-element.75) | copy-start | bytes 196612
  616.9 77.5 %copy-start.24 = (f32[8,8,8,32]{3,2,1,0:T(8,128)S(1)}, f32[8,8,8,32]{3,2,1,0:T(8,128)}, u32[]{:S(2)}) copy-start(f32[8,8,8,32]{3,2,1,0:T(8,128)} %get-tuple-element.101) | copy-start | bytes 196612
  616.9 77.5 %copy-start.25 = (f32[8,8,8,32]{3,2,1,0:T(8,128)S(1)}, f32[8,8,8,32]{3,2,1,0:T(8,128)}, u32[]{:S(2)}) copy-start(f32[8,8,8,32]{3,2,1,0:T(8,128)} %get-tuple-element.102) | copy-start | bytes 196612
  616.9 77.5 %copy-start.26 = (f32[8,8,8,32]{3,2,1,0:T(8,128)S(1)}, f32[8,8,8,32]{3,2,1,0:T(8,128)}, u32[]{:S(2)}) copy-start(f32[8,8,8,32]{3,2,1,0:T(8,128)} %get-tuple-element.103) | copy-start | bytes 196612
  616.9 77.5 %copy-start.27 = (f32[8,8,8,32]{3,2,1,0:T(8,128)S(1)}, f32[8,8,8,32]{3,2,1,0:T(8,128)}, u32[]{:S(2)}) copy-start(f32[8,8,8,32]{3,2,1,0:T(8,128)} %get-tuple-element.104) | copy-start | bytes 196612
  (34 other events, 812.3 us)
where the time goes:
time: 965 us; the launch traced here: 950 us
  local copies, waits for them, and re-layouts  437 us (45%)
  other arithmetic  264 us (27%)
  matrix products  196 us (20%)
  starting transfers between devices  52 us (5%)
    mul x5, local copies, waits for them, and re-layouts, transfer_matrix(): factor[:, None, None, :, None, None, :, None, None]  201 us
    reduce_sum x7, other arithmetic, near_field(): summed = summed + jnp.sum(kernel, axis=-1)  178 us
    dot_general x8, matrix products, translate(): jnp.dot(sources, operator_block.reshape(216 * reduced, reduced), precisio...  103 us
    slice x1, local copies, waits for them, and re-layouts, translate(): operator_grid[1 - parity_x:7 - parity_x, 1 - parity_y:7 - parity_y, 1 - p...  71.3 us
    mul x2, other arithmetic, transfer_matrix(): factor[:, None, None, :, None, None, :, None, None]  41.8 us
    unnamed x122, local copies, waits for them, and re-layouts  33.3 us
    dot_general x1, matrix products, far_field(): jnp.einsum('labg,als,bls,gls->ls', shaped, basis_x, basis_y, basis_z, pre...  30.6 us
    ppermute x8, starting transfers between devices, extended_2(): lax.ppermute(lax.slice_in_dim(block, 0, width, axis=dim), axis, backward)  29.6 us
  transfers between devices with their start and end apart: 16, of which 0 were waited for; matrix products, arithmetic and copies ran while one was open for 48% of the time, Pallas kernels for 0%

commit v1 on v0

v1 whole, which is shorter than its diff:
```python
import math

import jax
import jax.numpy as jnp
import numpy as np
from jax import lax
from jax.experimental import pallas as pl
from jax.experimental.pallas import tpu as pltpu
from jax.sharding import PartitionSpec as P

F32 = jnp.float32
BF16 = jnp.bfloat16
SOFTENING = 0.01
EXACT = lax.Precision.HIGHEST

FACE = 232
CORNER = 64
PACKED = FACE + 2 * CORNER
FACE_PAR, FACE_GRAND, FACE_NEAR = 128, 160, 168
COR_PAR, COR_GRAND, COR_NEAR = 32, 48, 56


def node_cos():
    return np.array(
        [[math.cos(math.pi * k * (2 * a + 1) / 16) for a in range(8)] for k in range(8)]
    )


def cheb_numpy(points):
    series = np.cos(np.arange(1, 8)[:, None] * np.arccos(points)[None, :])
    return 1 / 8 + 2 / 8 * node_cos()[1:].T @ series


def transfer_factor():
    nodes = np.cos(np.pi * (2 * np.arange(8) + 1) / 16)
    points = 0.5 * (nodes[None, :] + np.array([-1.0, 1.0])[:, None])
    weights = cheb_numpy(points.reshape(-1)).reshape(8, 2, 8)
    return weights.transpose(1, 2, 0)


def make_constants():
    factor = transfer_factor()
    lane = np.arange(128)
    lane_z, lane_x, lane_y = lane // 64, lane // 8 % 8, lane % 8
    lanes = np.zeros((4, 64, 128))
    for level in range(2):
        for which, coordinate in ((0, lane_x), (1, lane_y)):
            side = coordinate >> level & 1
            lanes[2 * level + which] = factor[side].transpose(1, 2, 0).reshape(64, 128)
    up_z = np.zeros((16, 8, 2, 16, 8))
    for block in range(16):
        for side in range(2):
            up_z[block, :, side, block, :] = factor[side].T
    up_z = up_z.reshape(128, 256)
    pick_par = np.zeros((64, 256))
    for x in range(4):
        for y in range(4):
            for z in range(4):
                pick_par[(x * 4 + y) * 4 + z, z % 2 * 128 + z // 2 * 64 + 2 * x * 8 + 2 * y] = 1
    pick_grand = np.zeros((8, 128))
    for x in range(2):
        for y in range(2):
            for z in range(2):
                pick_grand[(x * 2 + y) * 2 + z, z * 64 + 4 * x * 8 + 4 * y] = 1
    spread = np.kron(np.eye(8), np.ones((1, 32)))

    near_row = {}
    for x in range(8):
        for y in range(8):
            near_row[x, y] = x * 8 + y
    for y in range(8):
        near_row[-1, y] = 64 + y
        near_row[8, y] = 72 + y
        near_row[y, -1] = 80 + y
        near_row[y, 8] = 88 + y
    near_row[-1, -1], near_row[8, -1], near_row[-1, 8], near_row[8, 8] = 96, 97, 98, 99
    near_pick = np.zeros((256, 9, 128))
    for k in range(9):
        dx, dy = k // 3 - 1, k % 3 - 1
        for ln in range(128):
            row = near_row[int(lane_x[ln]) + dx, int(lane_y[ln]) + dy]
            near_pick[lane_z[ln] * 128 + row, k, ln] = 1
    near_pick = near_pick.reshape(256, 1152)

    leaf_row = {}
    for x in range(8):
        for y in range(8):
            leaf_row[x, y] = x * 8 + y
    for i in range(2):
        for y in range(8):
            leaf_row[i - 2, y] = 64 + i * 8 + y
            leaf_row[8 + i, y] = 80 + i * 8 + y
            leaf_row[y, i - 2] = 96 + y * 2 + i
            leaf_row[y, 8 + i] = 112 + y * 2 + i
        for j in range(2):
            leaf_row[i - 2, j - 2] = 128 + i * 2 + j
            leaf_row[8 + i, j - 2] = 136 + i * 2 + j
            leaf_row[i - 2, 8 + j] = 144 + i * 2 + j
            leaf_row[8 + i, 8 + j] = 152 + i * 2 + j
    leaf_pick = np.zeros((36, 16, 256))
    for v in range(36):
        sx, sy = v // 6 - 2, v % 6 - 2
        for r in range(16):
            leaf_pick[v, r, leaf_row[2 * (r // 4) + sx, 2 * (r % 4) + sy]] = 1
    leaf_pick = leaf_pick.reshape(576, 256)

    par_row = {}
    for x in range(4):
        for y in range(4):
            par_row[x, y] = x * 4 + y
    for i in range(2):
        for y in range(4):
            par_row[i - 2, y] = 16 + i * 4 + y
            par_row[4 + i, y] = 24 + i * 4 + y
            par_row[y, i - 2] = 32 + y * 2 + i
            par_row[y, 4 + i] = 40 + y * 2 + i
        for j in range(2):
            par_row[i - 2, j - 2] = 48 + i * 2 + j
            par_row[4 + i, j - 2] = 52 + i * 2 + j
            par_row[i - 2, 4 + j] = 56 + i * 2 + j
            par_row[4 + i, 4 + j] = 60 + i * 2 + j
    grand_row = {}
    order = [(0, 0), (-2, 0), (2, 0), (0, -2), (0, 2), (-2, -2), (2, -2), (-2, 2), (2, 2)]
    for n, (ox, oy) in enumerate(order):
        for i in range(2):
            for j in range(2):
                grand_row[ox + i, oy + j] = 128 + n * 4 + i * 2 + j
    small_pick = np.zeros((36, 3, 16, 256))
    for v in range(36):
        sx, sy = v // 6 - 2, v % 6 - 2
        for d in range(3):
            for r in range(8):
                zp = r // 4 + d - 1
                if 0 <= zp < 2:
                    row = par_row[2 * (r // 2 % 2) + sx, 2 * (r % 2) + sy]
                    small_pick[v, d, r, zp * 64 + row] = 1
            if d == 1:
                small_pick[v, d, 8, grand_row[sx, sy]] = 1
    small_pick = small_pick.reshape(1728, 256)

    place_leaf = np.zeros((128, 128))
    for z in range(2):
        for px in range(2):
            for py in range(2):
                for xp in range(4):
                    for yp in range(4):
                        row = ((z * 2 + px) * 2 + py) * 16 + xp * 4 + yp
                        place_leaf[row, z * 64 + (2 * xp + px) * 8 + 2 * yp + py] = 1
    place_small = np.zeros((3, 128, 128))
    for ln in range(128):
        z, x, y = int(lane_z[ln]), int(lane_x[ln]) >> 1, int(lane_y[ln]) >> 1
        for q in range(2):
            row = (((q * 2 + z) * 2 + x % 2) * 2 + y % 2) * 4 + x // 2 * 2 + y // 2
            place_small[q, row, ln] = 1
        place_small[2, 64 + ((x >> 1) * 2 + (y >> 1)) * 2 + z, ln] = 1

    def half(array):
        return np.asarray(array, np.float32).astype(jnp.bfloat16)

    return dict(
        lanes=np.asarray(lanes, np.float32),
        up_z=np.asarray(up_z, np.float32),
        down_z=np.asarray(up_z.T, np.float32),
        pick_par=np.asarray(pick_par, np.float32),
        pick_grand=np.asarray(pick_grand, np.float32),
        spread=half(spread),
        near_pick=half(near_pick),
        leaf_pick=half(leaf_pick),
        small_pick=half(small_pick),
        place_leaf=half(place_leaf),
        place_small=half(place_small),
    )


def mm(a, b):
    return jnp.dot(a, b, preferred_element_type=F32)


def split2(x):
    high = x.astype(BF16)
    return high, (x - high.astype(F32)).astype(BF16)


def split3(x):
    high = x.astype(BF16)
    rest = x - high.astype(F32)
    mid = rest.astype(BF16)
    return high, mid, (rest - mid.astype(F32)).astype(BF16)


def mm3(a, b):
    a_high, a_low = a
    b_high, b_low = b
    return mm(a_high, b_high) + (mm(a_high, b_low) + mm(a_low, b_high))


def lanes_first(block):
    return jnp.concatenate([block[:, :128], block[:, 128:]], axis=0).T


def basis(points):
    u = jnp.clip(2.0 * points - 1.0, -1.0, 1.0)
    series = [None, u]
    for _ in range(2, 8):
        before = series[-2] if len(series) > 2 else 1.0
        series.append(2.0 * u * series[-1] - before)
    table = node_cos()
    weights = [None] * 8
    for a in range(4):
        even = 0.125
        odd = None
        for k in range(1, 8):
            term = series[k] * np.float32(0.25 * table[k, a])
            if k % 2 == 0:
                even = even + term
            else:
                odd = term if odd is None else odd + term
        weights[a] = even + odd
        weights[7 - a] = even - odd
    return weights


def occupied_slots(counts_ref, spread_ref):
    limits = mm(counts_ref[...].astype(F32).astype(BF16), spread_ref[...])
    slot = lax.broadcasted_iota(jnp.int32, (64, 256), 1) & 31
    return jnp.where(slot.astype(F32) < limits, 1.0, 0.0)


def bcast(ref, row):
    return jnp.broadcast_to(ref[pl.ds(row, 1), :], (8, 128))


def mix_x(source, target, lanes_ref, which, up):
    for out in range(8):
        total = None
        for inner in range(8):
            row = inner * 8 + out if up else out * 8 + inner
            term = lanes_ref[which, row : row + 1, :] * source[inner * 64 : inner * 64 + 64, :]
            total = term if total is None else total + term
        if up:
            shift = 8 << (which // 2)
            total = total + pltpu.roll(total, 128 - shift, 1)
        target[out * 64 : out * 64 + 64, :] = total


def mix_y(source, target, lanes_ref, which, up):
    def one(a, carry):
        start = pl.multiple_of(a * 64, 64)
        rows = [source[pl.ds(start + 8 * b, 8), :] for b in range(8)]
        for out in range(8):
            total = None
            for inner in range(8):
                row = inner * 8 + out if up else out * 8 + inner
                term = lanes_ref[which, row : row + 1, :] * rows[inner]
                total = term if total is None else total + term
            if up:
                shift = 1 << (which // 2)
                total = total + pltpu.roll(total, 128 - shift, 1)
            target[pl.ds(start + 8 * out, 8), :] = total
        return carry

    lax.fori_loop(0, 8, one, 0)


def upward_kernel(
    pos, charges, counts, compress, lanes, up_z, pick_par, pick_grand, spread,
    leaf, par, grand, xs_low, xs_high, ys_low, ys_high, weighted,
    flat, basis_x, basis_y, basis_z, moments, work_a, work_b, parents,
):
    w = charges[...] * occupied_slots(counts, spread)
    weighted[...] = w
    for component in range(3):
        flat[component] = lanes_first(pos[component])
    flat[3] = lanes_first(w)

    def chunk(c, carry):
        rows = pl.ds(pl.multiple_of(c * 32, 32), 32)
        mass = flat[3, rows, :]
        for a, value in enumerate(basis(flat[0, rows, :])):
            basis_x[a * 32 : a * 32 + 32, :] = value
        for a, value in enumerate(basis(flat[1, rows, :])):
            basis_y[a * 32 : a * 32 + 32, :] = value * mass
        for a, value in enumerate(basis(flat[2, rows, :])):
            basis_z[pl.ds(a, 32, stride=8), :] = value
        for half in range(2):

            def slot(s, sums):
                along_z = basis_z[pl.ds(pl.multiple_of(s * 8, 8), 8), :]
                along_y = [bcast(basis_y, b * 32 + s) for b in range(8)]
                result = []
                for a in range(4):
                    part = bcast(basis_x, (half * 4 + a) * 32 + s) * along_z
                    for b in range(8):
                        result.append(sums[a * 8 + b] + part * along_y[b])
                return tuple(result)

            zero = jnp.zeros((8, 128), F32)
            sums = lax.fori_loop(0, 32, slot, (zero,) * 32)
            for n in range(32):
                moments[c, (half * 32 + n) * 8 : (half * 32 + n) * 8 + 8, :] = sums[n]
        return carry

    lax.fori_loop(0, 4, chunk, 0)
    compress_t = split2(compress[...].T)
    for c in range(4):
        small = mm3(compress_t, split2(moments[c])).T
        for z in range(2):
            leaf[pl.ds(c + 4 * z, 64, stride=8), :] = small[z * 64 : z * 64 + 64, :]

    step = split2(up_z[...])

    def join_z(low, high, target):
        for block in range(4):
            rows = slice(block * 128, block * 128 + 128)
            pair = jnp.concatenate([low[rows, :], high[rows, :]], axis=0)
            target[rows, :] = mm3(step, split2(pair))

    rough = []
    for q in range(2):
        join_z(moments.at[2 * q], moments.at[2 * q + 1], work_a)
        mix_x(work_a, work_b, lanes, 0, True)
        mix_y(work_b, parents.at[q], lanes, 1, True)
        rough.append(mm3(compress_t, split2(parents[q])).T)
    par[...] = jnp.dot(
        pick_par[...], jnp.concatenate(rough, axis=0), precision=EXACT, preferred_element_type=F32
    )
    join_z(parents.at[0], parents.at[1], work_a)
    mix_x(work_a, work_b, lanes, 2, True)
    mix_y(work_b, work_a, lanes, 3, True)
    rough = mm3(compress_t, split2(work_a[...])).T
    grand[...] = jnp.dot(pick_grand[...], rough, precision=EXACT, preferred_element_type=F32)

    def particle(component, cells, part):
        columns = slice(part * 128, part * 128 + 128)
        if component < 3:
            return pos[component, cells, columns]
        return weighted[cells, columns]

    for buffer, x0, px0, xn in ((xs_low, 0, 0, 0), (xs_high, 6, 2, 7)):
        buffer[0:128, :] = leaf[x0 * 64 : x0 * 64 + 128, :]
        buffer[FACE_PAR : FACE_PAR + 32, :] = par[px0 * 16 : px0 * 16 + 32, :]
        buffer[FACE_GRAND : FACE_GRAND + 8, :] = grand[...]
        for corner, y0, py0, yn in ((FACE, 0, 0, 0), (FACE + CORNER, 6, 2, 7)):
            for i in range(2):
                source = ((x0 + i) * 8 + y0) * 8
                buffer[corner + i * 16 : corner + i * 16 + 16, :] = leaf[source : source + 16, :]
                source = ((px0 + i) * 4 + py0) * 4
                target = corner + COR_PAR + i * 8
                buffer[target : target + 8, :] = par[source : source + 8, :]
            target = corner + COR_GRAND
            buffer[target : target + 8, :] = grand[...]
        for component in range(4):
            for part in range(2):
                row = 2 * component + part
                value = particle(component, slice(xn * 8, xn * 8 + 8), part)
                buffer[pl.ds(FACE_NEAR + row, 8, stride=8), :] = value
                for corner, yn in ((FACE, 0), (FACE + CORNER, 7)):
                    target = corner + COR_NEAR + row
                    buffer[target : target + 1, :] = value[yn : yn + 1, :]
    for buffer, y0, py0, yn in ((ys_low, 0, 0, 0), (ys_high, 6, 2, 7)):
        for x in range(8):
            source = (x * 8 + y0) * 8
            buffer[x * 16 : x * 16 + 16, :] = leaf[source : source + 16, :]
        for x in range(4):
            source = (x * 4 + py0) * 4
            target = FACE_PAR + x * 8
            buffer[target : target + 8, :] = par[source : source + 8, :]
        buffer[FACE_GRAND : FACE_GRAND + 8, :] = grand[...]
        for x in range(8):
            for component in range(4):
                for part in range(2):
                    value = particle(component, slice(x * 8 + yn, x * 8 + yn + 1), part)
                    target = FACE_NEAR + x * 8 + 2 * component + part
                    buffer[target : target + 1, :] = value


def near_kernel(
    pos, weighted, x_low, x_high, y_low, y_high, pick, near,
    columns, sources, squares, targets,
):
    columns[...] = jnp.zeros_like(columns)
    for component in range(4):
        for part in range(2):
            row = 2 * component + part
            lanes = slice(part * 128, part * 128 + 128)
            own = pos[component, :, lanes] if component < 3 else weighted[:, lanes]
            columns[row, 0:64, :] = own
            for n, buffer in enumerate((x_low, x_high, y_low, y_high)):
                columns[row, 64 + 8 * n : 72 + 8 * n, :] = buffer[
                    pl.ds(FACE_NEAR + row, 8, stride=8), :
                ]
            for n, buffer in enumerate((y_low, y_high)):
                for side in range(2):
                    source = FACE + side * CORNER + COR_NEAR + row
                    target = 96 + 2 * n + side
                    columns[row, target : target + 1, :] = buffer[source : source + 1, :]
    empty = jnp.zeros((32, 128), F32)
    for component in range(4):
        low = columns[2 * component].T
        high = columns[2 * component + 1].T
        left = jnp.concatenate([empty, low, high[0:32, :]], axis=0)
        right = jnp.concatenate([low[96:128, :], high, empty], axis=0)
        pieces = split3(jnp.concatenate([left, right], axis=1))
        for k in range(9):
            table = pick[:, k * 128 : k * 128 + 128]
            value = (mm(pieces[0], table) + mm(pieces[1], table)) + mm(pieces[2], table)
            if component == 3:
                sources[3, k] = value
                continue
            offset = (k // 3 - 1, k % 3 - 1, 0)[component] - 0.5
            value = value + offset
            if k == 4:
                targets[component] = value[32:160, :]
            sources[component, k] = -2.0 * value
            if component == 0:
                squares[k] = value * value + SOFTENING
            else:
                squares[k] = squares[k] + value * value

    slot = lax.broadcasted_iota(jnp.int32, (8, 128), 0)

    def chunk(c, carry):
        start = pl.multiple_of(c * 32, 32)
        groups = [
            [targets[component, pl.ds(start + 8 * g, 8), :] for component in range(3)]
            for g in range(4)
        ]
        flat = [t[0] * t[0] + t[1] * t[1] for t in groups]
        sums = (jnp.zeros((8, 128), F32),) * 4
        for dz in (-1, 0, 1):
            base = start + 32 * (1 + dz)
            high = [t[2] - float(dz) for t in groups]
            square = [f + h * h for f, h in zip(flat, high)]

            def block(k, sums, own, base=base, high=high, square=square):
                sums = list(sums)
                for s in range(32):
                    row = pl.ds(base + s, 1)
                    px = jnp.broadcast_to(sources[0, k, row, :], (8, 128))
                    py = jnp.broadcast_to(sources[1, k, row, :], (8, 128))
                    pz = jnp.broadcast_to(sources[2, k, row, :], (8, 128))
                    pw = jnp.broadcast_to(sources[3, k, row, :], (8, 128))
                    pq = jnp.broadcast_to(squares[k, row, :], (8, 128))
                    for g in range(4):
                        distance = (
                            (square[g] + pq)
                            + groups[g][0] * px
                            + (groups[g][1] * py + high[g] * pz)
                        )
                        term = pw * lax.rsqrt(distance)
                        if own and s // 8 == g:
                            term = jnp.where(slot == s % 8, 0.0, term)
                        sums[g] = sums[g] + term
                return tuple(sums)

            if dz == 0:
                sums = lax.fori_loop(
                    0, 8, lambda n, t: block(n + jnp.where(n >= 4, 1, 0), t, False), sums
                )
                sums = block(4, sums, True)
            else:
                sums = lax.fori_loop(0, 9, lambda n, t: block(n, t, False), sums)
        for g in range(4):
            near[pl.ds(start + 8 * g, 8), :] = sums[g]
        return carry

    lax.fori_loop(0, 4, chunk, 0)


ROW_STARTS = (0, 49, 98, 138, 178, 218, 267, 316)


def downward_kernel(
    pos, counts, near, leaf, par, grand, x_low, x_high, y_low, y_high, operators, expand,
    lanes, down_z, spread, leaf_pick, small_pick, place_leaf, place_small,
    out,
    weights, staged, small, leaf_high, leaf_low, small_high, small_low, right_high, right_low,
    sums, flat, basis_x, basis_y, basis_z, local, work_a, work_b, work_c, far, arrivals,
):
    copies = [
        pltpu.make_async_copy(
            operators.at[pl.ds(ROW_STARTS[n], ROW_STARTS[n + 1] - ROW_STARTS[n])],
            weights.at[pl.ds(ROW_STARTS[n], ROW_STARTS[n + 1] - ROW_STARTS[n])],
            arrivals.at[n],
        )
        for n in range(7)
    ]
    for copy in copies:
        copy.start()

    staged[...] = jnp.zeros_like(staged)
    small[...] = jnp.zeros_like(small)
    faces = (x_low, x_high, y_low, y_high)
    for z in range(8):
        columns = slice(z * 128, z * 128 + 128)
        staged[0:64, columns] = leaf[pl.ds(z, 64, stride=8), :]
        for n, buffer in enumerate(faces):
            target = 64 + 16 * n
            staged[target : target + 16, columns] = buffer[pl.ds(z, 16, stride=8), :]
        for n, buffer in enumerate((y_low, y_high)):
            for side in range(2):
                target = 128 + 16 * n + 8 * side
                source = FACE + side * CORNER + z
                staged[target : target + 4, columns] = buffer[pl.ds(source, 4, stride=8), :]
    for z in range(4):
        columns = slice(z % 2 * 128, z % 2 * 128 + 128)
        top = z // 2 * 64
        small[top : top + 16, columns] = par[pl.ds(z, 16, stride=4), :]
        for n, buffer in enumerate(faces):
            target = top + 16 + 8 * n
            small[target : target + 8, columns] = buffer[pl.ds(FACE_PAR + z, 8, stride=4), :]
        for n, buffer in enumerate((y_low, y_high)):
            for side in range(2):
                target = top + 48 + 8 * n + 4 * side
                source = FACE + side * CORNER + COR_PAR + z
                small[target : target + 4, columns] = buffer[pl.ds(source, 4, stride=4), :]
    for z in range(2):
        columns = slice(z * 128, z * 128 + 128)
        small[128:132, columns] = grand[pl.ds(z, 4, stride=2), :]
        for n, buffer in enumerate(faces):
            target = 132 + 4 * n
            small[target : target + 4, columns] = buffer[pl.ds(FACE_GRAND + z, 4, stride=2), :]
        for n, buffer in enumerate((y_low, y_high)):
            for side in range(2):
                target = 148 + 8 * n + 4 * side
                source = FACE + side * CORNER + COR_GRAND + z
                small[target : target + 4, columns] = buffer[pl.ds(source, 4, stride=2), :]

    blank = jnp.zeros((36, 16, 256), BF16)
    for target in (leaf_high, leaf_low):
        target[:, 0] = blank
        target[:, 5] = blank
    for zp in range(4):
        pieces = split2(staged[:, zp * 256 : zp * 256 + 256])
        for piece, target in zip(pieces, (leaf_high, leaf_low)):
            target[:, zp + 1] = mm(leaf_pick[...], piece).astype(BF16).reshape(36, 16, 256)
    for piece, target in zip(split2(small[...]), (small_high, small_low)):
        target[...] = mm(small_pick[...], piece).astype(BF16).reshape(36, 3, 16, 256)

    sums[...] = jnp.zeros_like(sums)

    def left(high, v, d):
        main, rest = (leaf_high, small_high) if high else (leaf_low, small_low)
        return jnp.concatenate(
            [main[v, pl.ds(d, 4)].reshape(64, 256), rest[v, d]], axis=0
        )

    def translate(dx, dy, xs, ys, base, beside):
        split = {}
        for n, dz in enumerate((-3, -2, 2, 3) if beside else range(-3, 4)):
            split[dz] = split2(weights[base + n])
        for d in range(3):
            for which, target in ((0, right_high), (1, right_low)):
                for source in range(2):
                    for side in range(2):
                        dz = 2 * (d - 1) + source - side
                        value = split[dz][which] if dz in split else jnp.zeros((128, 128), BF16)
                        target[
                            d,
                            source * 128 : source * 128 + 128,
                            side * 128 : side * 128 + 128,
                        ] = value
        total = None
        sides = [(px, py) for px in xs for py in ys]
        for d in range(3):
            if beside and d == 1:
                continue
            variants = [(px + dx + 2) * 6 + (py + dy + 2) for px, py in sides]
            upper = jnp.concatenate([left(True, v, d) for v in variants], axis=0)
            lower = jnp.concatenate([left(False, v, d) for v in variants], axis=0)
            term = (mm(upper, right_high[d]) + mm(lower, right_high[d])) + mm(upper, right_low[d])
            total = term if total is None else total + term
        for n, (px, py) in enumerate(sides):
            sums[px * 2 + py] = sums[px * 2 + py] + total[n * 80 : n * 80 + 80, :]

    both = (0, 1)
    for n, dx in enumerate(range(-3, 4)):
        copies[n].wait()
        start = ROW_STARTS[n]
        xs = (1,) if dx == -3 else (0,) if dx == 3 else both
        middle = abs(dx) <= 1
        translate(dx, -3, xs, (1,), start, False)
        if middle:
            translate(dx, -2, xs, both, start + 7, False)
            lax.fori_loop(
                0,
                3,
                lambda i, t: (translate(dx, i - 1, xs, both, start + 14 + 4 * i, True), t)[1],
                0,
            )
            translate(dx, 2, xs, both, start + 26, False)
            translate(dx, 3, xs, (0,), start + 33, False)
        else:
            lax.fori_loop(
                0,
                5,
                lambda i, t: (translate(dx, i - 2, xs, both, start + 7 + 7 * i, False), t)[1],
                0,
            )
            translate(dx, 3, xs, (0,), start + 42, False)

    grow = split2(expand[...].T)
    pairs = [(px, py) for px in both for py in both]

    def expanded(rows, place):
        flipped = split2(rows.T)
        placed = tuple(mm(piece, place).astype(BF16) for piece in flipped)
        return mm3(grow, placed)

    pieces = []
    for q in range(2):
        for z in range(2):
            for px, py in pairs:
                rows = slice(64 + 4 * z, 68 + 4 * z)
                pieces.append(sums[px * 2 + py, rows, q * 128 : q * 128 + 128] * 0.5)
    for px, py in pairs:
        for z in range(2):
            pieces.append(sums[px * 2 + py, 72:73, z * 128 : z * 128 + 128] * 0.25)
    pieces.append(jnp.zeros((56, 128), F32))
    coarse = jnp.concatenate(pieces, axis=0)
    step = split2(down_z[...])

    work_a[...] = expanded(coarse, place_small[2])
    mix_x(work_a, work_b, lanes, 2, False)
    mix_y(work_b, work_c, lanes, 3, False)

    for component in range(3):
        flat[component] = lanes_first(pos[component])

    for q in range(2):
        side = tuple(piece[q * 128 : q * 128 + 128, :] for piece in step)
        work_a[...] = expanded(coarse, place_small[q])
        for block in range(4):
            rows = slice(block * 128, block * 128 + 128)
            work_a[rows, :] = work_a[rows, :] + mm3(side, split2(work_c[rows, :]))
        mix_x(work_a, work_b, lanes, 0, False)
        mix_y(work_b, work_a, lanes, 1, False)
        for cz in range(2):
            rows = [
                sums[px * 2 + py, (q + 2 * z) * 16 : (q + 2 * z) * 16 + 16, cz * 128 : cz * 128 + 128]
                for z in range(2)
                for px, py in pairs
            ]
            side = tuple(piece[cz * 128 : cz * 128 + 128, :] for piece in step)
            local[2 * q + cz] = expanded(jnp.concatenate(rows, axis=0), place_leaf[...])
            for block in range(4):
                part = slice(block * 128, block * 128 + 128)
                local[2 * q + cz, part, :] = local[2 * q + cz, part, :] + mm3(
                    side, split2(work_a[part, :])
                )

    def chunk(c, carry):
        start = pl.multiple_of(c * 32, 32)
        rows = pl.ds(start, 32)
        for a, value in enumerate(basis(flat[0, rows, :])):
            basis_x[a * 32 : a * 32 + 32, :] = value
        for a, value in enumerate(basis(flat[1, rows, :])):
            basis_y[a * 32 : a * 32 + 32, :] = value
        for a, value in enumerate(basis(flat[2, rows, :])):
            basis_z[pl.ds(a, 32, stride=8), :] = value

        def slots(n, carry):
            first = 2 * n
            totals = [None, None]
            along_y = [[bcast(basis_y, b * 32 + first + j) for b in range(8)] for j in range(2)]
            for a in range(8):
                inner = [None, None]
                for b in range(8):
                    value = local[c, (a * 8 + b) * 8 : (a * 8 + b) * 8 + 8, :]
                    for j in range(2):
                        term = value * along_y[j][b]
                        inner[j] = term if inner[j] is None else inner[j] + term
                for j in range(2):
                    term = inner[j] * bcast(basis_x, a * 32 + first + j)
                    totals[j] = term if totals[j] is None else totals[j] + term
            for j in range(2):
                along_z = basis_z[pl.ds(pl.multiple_of((first + j) * 8, 8), 8), :]
                far[pl.ds(start + first + j, 1), :] = jnp.sum(
                    totals[j] * along_z, axis=0, keepdims=True
                )
            return carry

        lax.fori_loop(0, 16, slots, 0)
        return carry

    lax.fori_loop(0, 4, chunk, 0)
    total = (far[...] + near[...]).T
    occupied = occupied_slots(counts, spread)
    out[...] = jnp.concatenate([total[0:64, :], total[64:128, :]], axis=1) * occupied


def vmem(count):
    return [pl.BlockSpec(memory_space=pltpu.VMEM) for _ in range(count)]


def shaped(*dims):
    return jax.ShapeDtypeStruct(dims, F32)


def neighbours(low, high, axis):
    count = lax.axis_size(axis)
    up = [(i, i + 1) for i in range(count - 1)]
    down = [(target, source) for source, target in up]
    return lax.ppermute(high, axis, up), lax.ppermute(low, axis, down)


def per_device(positions, charges, counts, compress, operators, expand):
    const = {name: jnp.asarray(value) for name, value in make_constants().items()}
    pos = positions.reshape(3, 64, 256)
    cells = counts.reshape(64, 8)
    limit = pltpu.CompilerParams(vmem_limit_bytes=56 * 1024 * 1024)
    leaf, par, grand, xs_low, xs_high, ys_low, ys_high, weighted = pl.pallas_call(
        upward_kernel,
        out_shape=[
            shaped(512, 128), shaped(64, 128), shaped(8, 128),
            shaped(PACKED, 128), shaped(PACKED, 128), shaped(FACE, 128), shaped(FACE, 128),
            shaped(64, 256),
        ],
        in_specs=vmem(9),
        out_specs=vmem(8),
        scratch_shapes=[
            pltpu.VMEM((4, 128, 128), F32),
            pltpu.VMEM((256, 128), F32),
            pltpu.VMEM((256, 128), F32),
            pltpu.VMEM((256, 128), F32),
            pltpu.VMEM((4, 512, 128), F32),
            pltpu.VMEM((512, 128), F32),
            pltpu.VMEM((512, 128), F32),
            pltpu.VMEM((2, 512, 128), F32),
        ],
        compiler_params=limit,
        name="upward",
    )(
        pos, charges.reshape(64, 256), cells, compress, const["lanes"], const["up_z"],
        const["pick_par"], const["pick_grand"], const["spread"],
    )
    x_low, x_high = neighbours(xs_low, xs_high, "gx")
    first, second = slice(FACE, FACE + CORNER), slice(FACE + CORNER, PACKED)
    y_low, y_high = neighbours(
        jnp.concatenate([ys_low, x_low[first], x_high[first]], axis=0),
        jnp.concatenate([ys_high, x_low[second], x_high[second]], axis=0),
        "gy",
    )
    near = pl.pallas_call(
        near_kernel,
        out_shape=shaped(128, 128),
        in_specs=vmem(7),
        out_specs=vmem(1)[0],
        scratch_shapes=[
            pltpu.VMEM((8, 128, 128), F32),
            pltpu.VMEM((4, 9, 192, 128), F32),
            pltpu.VMEM((9, 192, 128), F32),
            pltpu.VMEM((3, 128, 128), F32),
        ],
        compiler_params=limit,
        name="near",
    )(pos, weighted, x_low, x_high, y_low, y_high, const["near_pick"])
    result = pl.pallas_call(
        downward_kernel,
        out_shape=shaped(64, 256),
        in_specs=vmem(10) + [pl.BlockSpec(memory_space=pl.ANY)] + vmem(8),
        out_specs=vmem(1)[0],
        scratch_shapes=[
            pltpu.VMEM((316, 128, 128), F32),
            pltpu.VMEM((256, 1024), F32),
            pltpu.VMEM((256, 256), F32),
            pltpu.VMEM((36, 6, 16, 256), BF16),
            pltpu.VMEM((36, 6, 16, 256), BF16),
            pltpu.VMEM((36, 3, 16, 256), BF16),
            pltpu.VMEM((36, 3, 16, 256), BF16),
            pltpu.VMEM((3, 256, 256), BF16),
            pltpu.VMEM((3, 256, 256), BF16),
            pltpu.VMEM((4, 80, 256), F32),
            pltpu.VMEM((3, 128, 128), F32),
            pltpu.VMEM((256, 128), F32),
            pltpu.VMEM((256, 128), F32),
            pltpu.VMEM((256, 128), F32),
            pltpu.VMEM((4, 512, 128), F32),
            pltpu.VMEM((512, 128), F32),
            pltpu.VMEM((512, 128), F32),
            pltpu.VMEM((512, 128), F32),
            pltpu.VMEM((128, 128), F32),
            pltpu.SemaphoreType.DMA((7,)),
        ],
        compiler_params=limit,
        name="downward",
    )(
        pos, cells, near, leaf, par, grand, x_low, x_high, y_low, y_high, operators, expand,
        const["lanes"], const["down_z"], const["spread"], const["leaf_pick"],
        const["small_pick"], const["place_leaf"], const["place_small"],
    )
    return result.reshape(8, 8, 256)


def solution(mesh):
    placed = (P(None, "gx", "gy", None), P("gx", "gy", None), P("gx", "gy", None), P(), P(), P())
    return jax.shard_map(
        per_device, mesh=mesh, in_specs=placed, out_specs=P("gx", "gy", None), check_vma=False
    )
```

time: 965 us -> 103 us (0.11); the launches traced: 950 us -> 101 us
  local copies, waits for them, and re-layouts: 437 us -> 0.68 us
  other arithmetic: 264 us -> 1.9 us
  matrix products: 196 us -> 0 us
  Pallas kernels: 0 us -> 76.5 us
  starting transfers between devices: 52 us -> 13.4 us
    mul x9 -> x0, local copies, waits for them, and re-layouts: 204 us -> none  [the longest x5 201 us: transfer_matrix(): factor[:, None, None, :, None, None, :, None, None]]
    dot_general x24 -> x0, matrix products: 196 us -> none  [the longest x8 103 us: translate(): jnp.dot(sources, operator_block.reshape(216 * reduced, reduced), precisio...]
    reduce_sum x7 -> x0, other arithmetic: 178 us -> none  [near_field(): summed = summed + jnp.sum(kernel, axis=-1)]
    pallas_call x0 -> x3, Pallas kernels: none -> 76.5 us  [the longest x1 38 us: per_device(): pl.pallas_call(downward_kernel, out_shape=shaped(64, 256), in_specs=vmem(...]
    slice x10 -> x2, local copies, waits for them, and re-layouts: 75 us -> 0.01 us  [the longest x1 0.01 us: per_device(): x_low[first]]
    mul x6 -> x0, other arithmetic: 43.9 us -> none  [the longest x2 41.8 us: transfer_matrix(): factor[:, None, None, :, None, None, :, None, None]]
    transpose x9 -> x0, local copies, waits for them, and re-layouts: 40.5 us -> none  [the longest x2 29.1 us: leaf_multipoles(): jnp.einsum('ls,als,bls,gls->labg', masses, basis_x, basis_y, basis_z, pre...]
    ppermute x16 -> x4, starting transfers between devices: 52 us -> 13.4 us  [neighbours(): return (lax.ppermute(high, axis, up), lax.ppermute(low, axis, down))]
  transfers between devices with their start and end apart: 16 -> 4, of which waited for: 0 -> 4; matrix products, arithmetic and copies ran while one was open for 48% -> 1% of each run, Pallas kernels for 0% -> 0%
where the time goes in v1:
time: 103 us; the launch traced here: 101 us
  Pallas kernels  76.5 us (74%)
  starting transfers between devices  13.4 us (13%)
  waiting for transfers between devices  8.72 us (8%)
  other arithmetic  1.9 us (2%)
    pallas_call x1, Pallas kernels, per_device(): pl.pallas_call(downward_kernel, out_shape=shaped(64, 256), in_specs=vmem(...  38 us
    pallas_call x1, Pallas kernels, per_device(): pl.pallas_call(near_kernel, out_shape=shaped(128, 128), in_specs=vmem(7),...  24.7 us
    pallas_call x1, Pallas kernels, per_device(): pl.pallas_call(upward_kernel, out_shape=[shaped(512, 128), shaped(64, 128...  13.8 us
    ppermute x4, starting transfers between devices, neighbours(): return (lax.ppermute(high, axis, up), lax.ppermute(low, axis, down))  13.4 us
    ppermute x4, waiting for transfers between devices, neighbours(): return (lax.ppermute(high, axis, up), lax.ppermute(low, axis, down))  8.72 us
  transfers between devices with their start and end apart: 4, of which 4 were waited for; matrix products, arithmetic and copies ran while one was open for 1% of the time, Pallas kernels for 0%

profile of v1, /device:TPU:41, one launch (start us, length us, event | category | flops | bytes accessed | tf_op | source)
XLA Modules:
  0.0 101.4 jit_solution(9813577610663175684)
XLA Ops:
  0.0 13.8 %upward.1 = (f32[512,128]{1,0:T(8,128)}, f32[64,128]{1,0:T(8,128)}, f32[8,128]{1,0:T(8,128)}, f32[360,128]{1,0:T(8,128)}, f32[360,128]{1,0:T(8,128)}, /*index=5*...) custom-call(f32[3,64,256]{2,1,0:T(8,128)} %bitcast.4, f32[64,256]{1,0:T(8,128)} %bitcast.9, s32[64,8]{1,0:T(8,128)} %bitcast.7, ...), custom_call_target="tpu_custom_call" | custom-call | tf_op jit(solution)/shard_map/upward/pallas_call | solution.py:712
  13.8 4.1 %collective-permute-start = (f32[360,128]{1,0:T(8,128)}, f32[360,128]{1,0:T(8,128)S(1)}, u32[]{:S(2)}, u32[]{:S(2)}) collective-permute-start(f32[360,128]{1,0:T(8,128)} %get-tuple-element.14), channel_id=1, source_target_pairs={{0,16},{16,32},{32,48},{48,64},{64,80},{80,96},{96,112},{1,17},{17... | collective-permute-start | bytes 552968 | tf_op jit(solution)/shard_map/ppermute | solution.py:704
  17.9 1.9 %collective-permute-start.1 = (f32[360,128]{1,0:T(8,128)}, f32[360,128]{1,0:T(8,128)S(1)}, u32[]{:S(2)}, u32[]{:S(2)}) collective-permute-start(f32[360,128]{1,0:T(8,128)} %get-tuple-element.15), channel_id=1, source_target_pairs={{16,0},{32,16},{48,32},{64,48},{80,64},{96,80},{112,96},{17,1},{33... | collective-permute-start | bytes 552968 | tf_op jit(solution)/shard_map/ppermute | solution.py:704
  19.8 0.8 collective-permute-done.x_low
  20.6 0.0 copy-start
  20.6 4.3 %collective-permute-done.1.x_high = f32[360,128]{1,0:T(8,128)S(1)} collective-permute-done((f32[360,128]{1,0:T(8,128)}, f32[360,128]{1,0:T(8,128)S(1)}, u32[]{:S(2)}, u32[]{:S(2)}) %collective-permute-start.1) | collective-permute-done | bytes 184352 | tf_op jit(solution)/shard_map/ppermute | solution.py:704
  24.9 0.0 copy-start.1
  24.9 1.0 pad_maximum_fusion
  25.9 3.1 %collective-permute-start.2 = (f32[360,128]{1,0:T(8,128)S(1)}, f32[360,128]{1,0:T(8,128)S(1)}, u32[]{:S(2)}, u32[]{:S(2)}) collective-permute-start(f32[360,128]{1,0:T(8,128)S(1)} %pad_maximum_fusion), channel_id=1, source_target_pairs={{0,1},{1,2},{2,3},{3,4},{4,5},{5,6},{6,7},{7,8},{8,9},{9,10},{10,1... | collective-permute-start | bytes 552968 | tf_op jit(solution)/shard_map/ppermute | solution.py:704
  29.0 0.9 pad_maximum_fusion.1
  30.0 4.3 %collective-permute-start.3 = (f32[360,128]{1,0:T(8,128)S(1)}, f32[360,128]{1,0:T(8,128)S(1)}, u32[]{:S(2)}, u32[]{:S(2)}) collective-permute-start(f32[360,128]{1,0:T(8,128)S(1)} %pad_maximum_fusion.1), channel_id=1, source_target_pairs={{1,0},{2,1},{3,2},{4,3},{5,4},{6,5},{7,6},{8,7},{9,8},{10,9},{11,1... | collective-permute-start | bytes 552968 | tf_op jit(solution)/shard_map/ppermute | solution.py:704
  34.2 0.9 collective-permute-done.2.y_low
  35.2 0.0 copy-start.2
  35.2 2.7 %collective-permute-done.3.y_high = f32[360,128]{1,0:T(8,128)S(1)} collective-permute-done((f32[360,128]{1,0:T(8,128)S(1)}, f32[360,128]{1,0:T(8,128)S(1)}, u32[]{:S(2)}, u32[]{:S(2)}) %collective-permute-start.3) | collective-permute-done | bytes 184352 | tf_op jit(solution)/shard_map/ppermute | solution.py:704
  37.8 0.0 copy-start.3
  37.8 0.0 copy-done
  37.8 0.0 copy-done.1
  37.8 0.0 copy-done.2
  37.9 0.7 copy-done.3
  38.5 24.7 %near.1 = f32[128,128]{1,0:T(8,128)} custom-call(f32[3,64,256]{2,1,0:T(8,128)} %bitcast.5, f32[64,256]{1,0:T(8,128)} %get-tuple-element.13.weighted, f32[360,128]{1,0:T(8,128)} %copy-done, f32[360,128]{1,0:T(8,128)} %copy-done.1, f32[360,128]{1,0:T(8,128)} %copy-done.2, f32[360,128]{1,0:T(8,128)} %copy-done.3, bf16[256,1152]{1,0:T(8,128)(2,1)} %constant.28.clone.pick), custom_call_target="tpu_custom_call" | custom-call | tf_op jit(solution)/shard_map/near/pallas_call | solution.py:744
  63.2 38.0 %downward.1 = f32[64,256]{1,0:T(8,128)} custom-call(f32[3,64,256]{2,1,0:T(8,128)} %bitcast.6, s32[64,8]{1,0:T(8,128)} %bitcast.8, f32[128,128]{1,0:T(8,128)} %near.1, f32[512,128]{1,0:T(8,128)} %get-tuple-element.18.leaf, f32[64,128]{1,0:T(8,128)} %get-tuple-element.19.par, f32[8,128]{1,0:T(8,128)} %get-tuple-element.20.grand, f32[360,128]{1,0:T(8,128)} %copy-done, ...), custom_call_target="tpu_custom_call" | custom-call | tf_op jit(solution)/shard_map/downward/pallas_call | solution.py:758
  (2 shorter events, 0.0 us)
Async XLA Ops:
  13.8 6.9 %collective-permute-start = (f32[360,128]{1,0:T(8,128)}, f32[360,128]{1,0:T(8,128)S(1)}, u32[]{:S(2)}, u32[]{:S(2)}) collective-permute-start(f32[360,128]{1,0:T(8,128)} %get-tuple-element.14), channel_id=1, source_target_pairs={{0,16},{16,32},{32,48},{48,64},{64,80},{80,96},{96,112},{1,17},{17... | collective-permute-start | bytes 552968 | tf_op jit(solution)/shard_map/ppermute | solution.py:704
  17.9 7.1 %collective-permute-start.1 = (f32[360,128]{1,0:T(8,128)}, f32[360,128]{1,0:T(8,128)S(1)}, u32[]{:S(2)}, u32[]{:S(2)}) collective-permute-start(f32[360,128]{1,0:T(8,128)} %get-tuple-element.15), channel_id=1, source_target_pairs={{16,0},{32,16},{48,32},{64,48},{80,64},{96,80},{112,96},{17,1},{33... | collective-permute-start | bytes 552968 | tf_op jit(solution)/shard_map/ppermute | solution.py:704
  20.6 17.2 %copy-start = (f32[360,128]{1,0:T(8,128)}, f32[360,128]{1,0:T(8,128)S(1)}, u32[]{:S(2)}) copy-start(f32[360,128]{1,0:T(8,128)S(1)} %collective-permute-done.x_low) | copy-start | bytes 552964
  24.9 12.9 %copy-start.1 = (f32[360,128]{1,0:T(8,128)}, f32[360,128]{1,0:T(8,128)S(1)}, u32[]{:S(2)}) copy-start(f32[360,128]{1,0:T(8,128)S(1)} %collective-permute-done.1.x_high) | copy-start | bytes 552964
  25.9 9.2 %collective-permute-start.2 = (f32[360,128]{1,0:T(8,128)S(1)}, f32[360,128]{1,0:T(8,128)S(1)}, u32[]{:S(2)}, u32[]{:S(2)}) collective-permute-start(f32[360,128]{1,0:T(8,128)S(1)} %pad_maximum_fusion), channel_id=1, source_target_pairs={{0,1},{1,2},{2,3},{3,4},{4,5},{5,6},{6,7},{7,8},{8,9},{9,10},{10,1... | collective-permute-start | bytes 552968 | tf_op jit(solution)/shard_map/ppermute | solution.py:704
  30.0 7.9 %collective-permute-start.3 = (f32[360,128]{1,0:T(8,128)S(1)}, f32[360,128]{1,0:T(8,128)S(1)}, u32[]{:S(2)}, u32[]{:S(2)}) collective-permute-start(f32[360,128]{1,0:T(8,128)S(1)} %pad_maximum_fusion.1), channel_id=1, source_target_pairs={{1,0},{2,1},{3,2},{4,3},{5,4},{6,5},{7,6},{8,7},{9,8},{10,9},{11,1... | collective-permute-start | bytes 552968 | tf_op jit(solution)/shard_map/ppermute | solution.py:704
  35.2 2.7 %copy-start.2 = (f32[360,128]{1,0:T(8,128)}, f32[360,128]{1,0:T(8,128)S(1)}, u32[]{:S(2)}) copy-start(f32[360,128]{1,0:T(8,128)S(1)} %collective-permute-done.2.y_low) | copy-start | bytes 552964
  37.8 0.7 copy-start.3

commit v2 on v1

--- a/solution.py
+++ b/solution.py
@@ -295,7 +295,7 @@
                 return tuple(result)
 
             zero = jnp.zeros((8, 128), F32)
-            sums = lax.fori_loop(0, 32, slot, (zero,) * 32)
+            sums = lax.fori_loop(0, 32, slot, (zero,) * 32, unroll=4)
             for n in range(32):
                 moments[c, (half * 32 + n) * 8 : (half * 32 + n) * 8 + 8, :] = sums[n]
         return carry
@@ -374,10 +374,7 @@
                     buffer[target : target + 1, :] = value
 
 
-def near_kernel(
-    pos, weighted, x_low, x_high, y_low, y_high, pick, near,
-    columns, sources, squares, targets,
-):
+def stage_columns(columns, pos, weighted, x_faces, y_faces):
     columns[...] = jnp.zeros_like(columns)
     for component in range(4):
         for part in range(2):
@@ -385,15 +382,18 @@
             lanes = slice(part * 128, part * 128 + 128)
             own = pos[component, :, lanes] if component < 3 else weighted[:, lanes]
             columns[row, 0:64, :] = own
-            for n, buffer in enumerate((x_low, x_high, y_low, y_high)):
+            for n, buffer in enumerate((*x_faces, *y_faces)):
                 columns[row, 64 + 8 * n : 72 + 8 * n, :] = buffer[
                     pl.ds(FACE_NEAR + row, 8, stride=8), :
                 ]
-            for n, buffer in enumerate((y_low, y_high)):
+            for n, buffer in enumerate(y_faces):
                 for side in range(2):
                     source = FACE + side * CORNER + COR_NEAR + row
                     target = 96 + 2 * n + side
                     columns[row, target : target + 1, :] = buffer[source : source + 1, :]
+
+
+def stage_sources(columns, pick, shifts, sources, squares):
     empty = jnp.zeros((32, 128), F32)
     for component in range(4):
         low = columns[2 * component].T
@@ -401,81 +401,103 @@
         left = jnp.concatenate([empty, low, high[0:32, :]], axis=0)
         right = jnp.concatenate([low[96:128, :], high, empty], axis=0)
         pieces = split3(jnp.concatenate([left, right], axis=1))
-        for k in range(9):
+        for n, k in enumerate(shifts):
             table = pick[:, k * 128 : k * 128 + 128]
             value = (mm(pieces[0], table) + mm(pieces[1], table)) + mm(pieces[2], table)
             if component == 3:
-                sources[3, k] = value
+                sources[3, n] = value
                 continue
             offset = (k // 3 - 1, k % 3 - 1, 0)[component] - 0.5
             value = value + offset
-            if k == 4:
-                targets[component] = value[32:160, :]
-            sources[component, k] = -2.0 * value
+            sources[component, n] = -2.0 * value
             if component == 0:
-                squares[k] = value * value + SOFTENING
+                squares[n] = value * value + SOFTENING
             else:
-                squares[k] = squares[k] + value * value
-
+                squares[n] = squares[n] + value * value
+
+
+def pair_steps(targets, start, dz, sources, squares, n, base, count, own, sums):
+    groups = [
+        [targets[component, pl.ds(start + 8 * g, 8), :] for component in range(3)]
+        for g in range(4)
+    ]
+    high = [t[2] - dz for t in groups]
+    square = [t[0] * t[0] + t[1] * t[1] + h * h for t, h in zip(groups, high)]
     slot = lax.broadcasted_iota(jnp.int32, (8, 128), 0)
+    for s in range(count):
+        row = pl.ds(base + s, 1)
+        px = jnp.broadcast_to(sources[0, n, row, :], (8, 128))
+        py = jnp.broadcast_to(sources[1, n, row, :], (8, 128))
+        pz = jnp.broadcast_to(sources[2, n, row, :], (8, 128))
+        pw = jnp.broadcast_to(sources[3, n, row, :], (8, 128))
+        pq = jnp.broadcast_to(squares[n, row, :], (8, 128))
+        for g in range(4):
+            distance = (square[g] + pq) + groups[g][0] * px + (groups[g][1] * py + high[g] * pz)
+            term = pw * lax.rsqrt(distance)
+            if own and s // 8 == g:
+                term = jnp.where(slot == s % 8, 0.0, term)
+            sums[g] = term if sums[g] is None else sums[g] + term
+        yield
+
+
+def pair_sums(*arguments):
+    sums = [None] * 4
+    for _ in pair_steps(*arguments, sums):
+        pass
+    return sums
+
+
+def near_part(shifts, pos, weighted, x_faces, pick, near, before, columns, sources, squares, targets):
+    stage_columns(columns, pos, weighted, x_faces, ())
+    stage_sources(columns, pick, shifts, sources, squares)
+    for component in range(3):
+        targets[component] = lanes_first(pos[component]) - 0.5
 
     def chunk(c, carry):
         start = pl.multiple_of(c * 32, 32)
-        groups = [
-            [targets[component, pl.ds(start + 8 * g, 8), :] for component in range(3)]
-            for g in range(4)
-        ]
-        flat = [t[0] * t[0] + t[1] * t[1] for t in groups]
-        sums = (jnp.zeros((8, 128), F32),) * 4
+        for g in range(4):
+            rows = pl.ds(start + 8 * g, 8)
+            near[rows, :] = jnp.zeros((8, 128), F32) if before is None else before[rows, :]
         for dz in (-1, 0, 1):
-            base = start + 32 * (1 + dz)
-            high = [t[2] - float(dz) for t in groups]
-            square = [f + h * h for f, h in zip(flat, high)]
-
-            def block(k, sums, own, base=base, high=high, square=square):
-                sums = list(sums)
-                for s in range(32):
-                    row = pl.ds(base + s, 1)
-                    px = jnp.broadcast_to(sources[0, k, row, :], (8, 128))
-                    py = jnp.broadcast_to(sources[1, k, row, :], (8, 128))
-                    pz = jnp.broadcast_to(sources[2, k, row, :], (8, 128))
-                    pw = jnp.broadcast_to(sources[3, k, row, :], (8, 128))
-                    pq = jnp.broadcast_to(squares[k, row, :], (8, 128))
-                    for g in range(4):
-                        distance = (
-                            (square[g] + pq)
-                            + groups[g][0] * px
-                            + (groups[g][1] * py + high[g] * pz)
-                        )
-                        term = pw * lax.rsqrt(distance)
-                        if own and s // 8 == g:
-                            term = jnp.where(slot == s % 8, 0.0, term)
-                        sums[g] = sums[g] + term
-                return tuple(sums)
-
-            if dz == 0:
-                sums = lax.fori_loop(
-                    0, 8, lambda n, t: block(n + jnp.where(n >= 4, 1, 0), t, False), sums
+            for n, k in enumerate(shifts):
+                sums = pair_sums(
+                    targets, start, float(dz), sources, squares, n,
+                    pl.multiple_of(start + 32 * (1 + dz), 32), 32, k == 4 and dz == 0,
                 )
-                sums = block(4, sums, True)
-            else:
-                sums = lax.fori_loop(0, 9, lambda n, t: block(n, t, False), sums)
-        for g in range(4):
-            near[pl.ds(start + 8 * g, 8), :] = sums[g]
+                for g in range(4):
+                    rows = pl.ds(start + 8 * g, 8)
+                    near[rows, :] = near[rows, :] + sums[g]
         return carry
 
     lax.fori_loop(0, 4, chunk, 0)
 
 
+def near_own_kernel(pos, weighted, pick, near, columns, sources, squares, targets):
+    near_part((4,), pos, weighted, (), pick, near, None, columns, sources, squares, targets)
+
+
+def near_x_kernel(
+    pos, weighted, x_low, x_high, pick, before, near, columns, sources, squares, targets
+):
+    near_part(
+        (1, 7), pos, weighted, (x_low, x_high), pick, near, before,
+        columns, sources, squares, targets,
+    )
+
+
+SIDEWAYS = (0, 2, 3, 5, 6, 8)
+
+
 ROW_STARTS = (0, 49, 98, 138, 178, 218, 267, 316)
 
 
 def downward_kernel(
-    pos, counts, near, leaf, par, grand, x_low, x_high, y_low, y_high, operators, expand,
-    lanes, down_z, spread, leaf_pick, small_pick, place_leaf, place_small,
+    pos, weighted, counts, before, leaf, par, grand, x_low, x_high, y_low, y_high, operators,
+    expand, lanes, down_z, spread, near_pick, leaf_pick, small_pick, place_leaf, place_small,
     out,
     weights, staged, small, leaf_high, leaf_low, small_high, small_low, right_high, right_low,
-    sums, flat, basis_x, basis_y, basis_z, local, work_a, work_b, work_c, far, arrivals,
+    sums, flat, basis_x, basis_y, basis_z, local, work_a, work_b, work_c, far,
+    near, columns, sources, squares, targets, arrivals,
 ):
     copies = [
         pltpu.make_async_copy(
@@ -487,6 +509,23 @@
     ]
     for copy in copies:
         copy.start()
+
+    near[...] = before[...]
+    stage_columns(columns, pos, weighted, (x_low, x_high), (y_low, y_high))
+    stage_sources(columns, near_pick, SIDEWAYS, sources, squares)
+    for component in range(3):
+        flat[component] = lanes_first(pos[component])
+        targets[component] = flat[component] - 0.5
+
+    def unit_steps(unit, chunks, results):
+        level = unit // 12
+        dz = (level - 1).astype(F32) if isinstance(level, jax.Array) else float(level - 1)
+        for c in chunks:
+            base = pl.multiple_of(32 * c + 32 * level + 16 * (unit % 2), 16)
+            results[c] = [None] * 4
+            yield from pair_steps(
+                targets, 32 * c, dz, sources, squares, unit % 12 // 2, base, 16, False, results[c]
+            )
 
     staged[...] = jnp.zeros_like(staged)
     small[...] = jnp.zeros_like(small)
@@ -545,59 +584,94 @@
             [main[v, pl.ds(d, 4)].reshape(64, 256), rest[v, d]], axis=0
         )
 
-    def translate(dx, dy, xs, ys, base, beside):
+    def translate(dx, dy, xs, ys, base, beside, unit, chunks):
         split = {}
         for n, dz in enumerate((-3, -2, 2, 3) if beside else range(-3, 4)):
             split[dz] = split2(weights[base + n])
+        none = jnp.zeros((128, 128), BF16)
+        right = {}
         for d in range(3):
-            for which, target in ((0, right_high), (1, right_low)):
-                for source in range(2):
-                    for side in range(2):
-                        dz = 2 * (d - 1) + source - side
-                        value = split[dz][which] if dz in split else jnp.zeros((128, 128), BF16)
-                        target[
-                            d,
-                            source * 128 : source * 128 + 128,
-                            side * 128 : side * 128 + 128,
-                        ] = value
-        total = None
+            for which in range(2):
+                right[d, which] = jnp.concatenate(
+                    [
+                        jnp.concatenate(
+                            [
+                                split[2 * (d - 1) + source - side][which]
+                                if 2 * (d - 1) + source - side in split
+                                else none
+                                for side in range(2)
+                            ],
+                            axis=1,
+                        )
+                        for source in range(2)
+                    ],
+                    axis=0,
+                )
+        pass
         sides = [(px, py) for px in xs for py in ys]
-        for d in range(3):
-            if beside and d == 1:
-                continue
-            variants = [(px + dx + 2) * 6 + (py + dy + 2) for px, py in sides]
+        variants = [(px + dx + 2) * 6 + (py + dy + 2) for px, py in sides]
+        jobs = []
+        for d in (0, 2) if beside else (0, 1, 2):
             upper = jnp.concatenate([left(True, v, d) for v in variants], axis=0)
             lower = jnp.concatenate([left(False, v, d) for v in variants], axis=0)
-            term = (mm(upper, right_high[d]) + mm(lower, right_high[d])) + mm(upper, right_low[d])
+            jobs += [(jnp.concatenate([upper, lower], axis=0), right[d, 0]), (upper, right[d, 1])]
+        results = {}
+        steps = unit_steps(unit, chunks, results)
+        todo = 16 * len(chunks)
+        done = 0
+        total = None
+        size = 80 * len(sides)
+        for n, (a, b) in enumerate(jobs):
+            term = mm(a, b)
+            if a.shape[0] > size:
+                term = term[:size] + term[size:]
             total = term if total is None else total + term
+            while done < todo * (n + 1) // len(jobs):
+                next(steps)
+                done += 1
         for n, (px, py) in enumerate(sides):
             sums[px * 2 + py] = sums[px * 2 + py] + total[n * 80 : n * 80 + 80, :]
+        for c in chunks:
+            for g in range(4):
+                rows = slice(32 * c + 8 * g, 32 * c + 8 * g + 8)
+                near[rows, :] = near[rows, :] + results[c][g]
 
     both = (0, 1)
+    every = (0, 1, 2, 3)
+    unit = 0
     for n, dx in enumerate(range(-3, 4)):
         copies[n].wait()
         start = ROW_STARTS[n]
         xs = (1,) if dx == -3 else (0,) if dx == 3 else both
         middle = abs(dx) <= 1
-        translate(dx, -3, xs, (1,), start, False)
+        outer = abs(dx) == 3
+        low, high = ((0,), (1,)) if dx == -3 else ((2,), (3,)) if dx == 3 else ((0, 1), (2, 3))
+        row = 35 if outer else 30 + dx + 2
+        translate(dx, -3, xs, (1,), start, False, row, low)
         if middle:
-            translate(dx, -2, xs, both, start + 7, False)
-            lax.fori_loop(
-                0,
-                3,
-                lambda i, t: (translate(dx, i - 1, xs, both, start + 14 + 4 * i, True), t)[1],
-                0,
-            )
-            translate(dx, 2, xs, both, start + 26, False)
-            translate(dx, 3, xs, (0,), start + 33, False)
+            translate(dx, -2, xs, both, start + 7, False, unit, every)
+
+            def step(i, carry, dx=dx, xs=xs, start=start):
+                place = 16 + 3 * (dx + 1) + i
+                translate(dx, i - 1, xs, both, start + 14 + 4 * i, True, place, every)
+                return carry
+
+            lax.fori_loop(0, 3, step, 0)
+            translate(dx, 2, xs, both, start + 26, False, unit + 1, every)
+            unit += 2
+            last = start + 33
         else:
-            lax.fori_loop(
-                0,
-                5,
-                lambda i, t: (translate(dx, i - 2, xs, both, start + 7 + 7 * i, False), t)[1],
-                0,
-            )
-            translate(dx, 3, xs, (0,), start + 42, False)
+            chunks = ((0, 1) if dx < 0 else (2, 3)) if outer else every
+
+            def step(i, carry, dx=dx, xs=xs, start=start, unit=unit, chunks=chunks, outer=outer):
+                place = 25 + i if outer else unit + i
+                translate(dx, i - 2, xs, both, start + 7 + 7 * i, False, place, chunks)
+                return carry
+
+            lax.fori_loop(0, 5, step, 0)
+            unit += 0 if outer else 5
+            last = start + 42
+        translate(dx, 3, xs, (0,), last, False, row, high)
 
     grow = split2(expand[...].T)
     pairs = [(px, py) for px in both for py in both]
@@ -623,9 +697,6 @@
     work_a[...] = expanded(coarse, place_small[2])
     mix_x(work_a, work_b, lanes, 2, False)
     mix_y(work_b, work_c, lanes, 3, False)
-
-    for component in range(3):
-        flat[component] = lanes_first(pos[component])
 
     for q in range(2):
         side = tuple(piece[q * 128 : q * 128 + 128, :] for piece in step)
@@ -680,7 +751,7 @@
                 )
             return carry
 
-        lax.fori_loop(0, 16, slots, 0)
+        lax.fori_loop(0, 16, slots, 0, unroll=2)
         return carry
 
     lax.fori_loop(0, 4, chunk, 0)
@@ -735,6 +806,25 @@
         const["pick_par"], const["pick_grand"], const["spread"],
     )
     x_low, x_high = neighbours(xs_low, xs_high, "gx")
+    def near_scratch(count):
+        return [
+            pltpu.VMEM((8, 128, 128), F32),
+            pltpu.VMEM((4, count, 192, 128), F32),
+            pltpu.VMEM((count, 192, 128), F32),
+            pltpu.VMEM((3, 128, 128), F32),
+        ]
+
+    near_own = pl.pallas_call(
+        near_own_kernel,
+        out_shape=shaped(128, 128),
+        in_specs=vmem(3),
+        out_specs=vmem(1)[0],
+        scratch_shapes=near_scratch(1),
+        compiler_params=limit,
+        cost_estimate=pl.CostEstimate(flops=10**7, bytes_accessed=10**7, transcendentals=0),
+        name="near_own",
+    )(pos, weighted, const["near_pick"])
+    near_own, x_low, x_high = lax.optimization_barrier((near_own, x_low, x_high))
     first, second = slice(FACE, FACE + CORNER), slice(FACE + CORNER, PACKED)
     y_low, y_high = neighbours(
         jnp.concatenate([ys_low, x_low[first], x_high[first]], axis=0),
@@ -742,23 +832,19 @@
         "gy",
     )
     near = pl.pallas_call(
-        near_kernel,
+        near_x_kernel,
         out_shape=shaped(128, 128),
-        in_specs=vmem(7),
+        in_specs=vmem(6),
         out_specs=vmem(1)[0],
-        scratch_shapes=[
-            pltpu.VMEM((8, 128, 128), F32),
-            pltpu.VMEM((4, 9, 192, 128), F32),
-            pltpu.VMEM((9, 192, 128), F32),
-            pltpu.VMEM((3, 128, 128), F32),
-        ],
+        scratch_shapes=near_scratch(2),
         compiler_params=limit,
-        name="near",
-    )(pos, weighted, x_low, x_high, y_low, y_high, const["near_pick"])
+        cost_estimate=pl.CostEstimate(flops=2 * 10**7, bytes_accessed=2 * 10**7, transcendentals=0),
+        name="near_x",
+    )(pos, weighted, x_low, x_high, const["near_pick"], near_own)
     result = pl.pallas_call(
         downward_kernel,
         out_shape=shaped(64, 256),
-        in_specs=vmem(10) + [pl.BlockSpec(memory_space=pl.ANY)] + vmem(8),
+        in_specs=vmem(11) + [pl.BlockSpec(memory_space=pl.ANY)] + vmem(9),
         out_specs=vmem(1)[0],
         scratch_shapes=[
             pltpu.VMEM((316, 128, 128), F32),
@@ -780,13 +866,15 @@
             pltpu.VMEM((512, 128), F32),
             pltpu.VMEM((512, 128), F32),
             pltpu.VMEM((128, 128), F32),
+            pltpu.VMEM((128, 128), F32),
+            *near_scratch(6),
             pltpu.SemaphoreType.DMA((7,)),
         ],
         compiler_params=limit,
         name="downward",
     )(
-        pos, cells, near, leaf, par, grand, x_low, x_high, y_low, y_high, operators, expand,
-        const["lanes"], const["down_z"], const["spread"], const["leaf_pick"],
+        pos, weighted, cells, near, leaf, par, grand, x_low, x_high, y_low, y_high, operators, expand,
+        const["lanes"], const["down_z"], const["spread"], const["near_pick"], const["leaf_pick"],
         const["small_pick"], const["place_leaf"], const["place_small"],
     )
     return result.reshape(8, 8, 256)

time: 103 us -> 86.7 us (0.84); the launches traced: 101 us -> 86.4 us
  waiting for transfers between devices: 8.72 us -> 0.65 us
  Pallas kernels: 76.5 us -> 69.4 us
    pallas_call x1 -> x2, Pallas kernels: 24.7 us -> 11.7 us  [the longest x1 7.2 us: per_device(): pl.pallas_call(near_x_kernel, out_shape=shaped(128, 128), in_specs=vmem(6...]
    pallas_call x1, Pallas kernels: 38 us -> 46.4 us  [per_device(): pl.pallas_call(downward_kernel, out_shape=shaped(64, 256), in_specs=vmem(...]
    ppermute x4, waiting for transfers between devices: 8.72 us -> 0.65 us  [neighbours(): return (lax.ppermute(high, axis, up), lax.ppermute(low, axis, down))]
    pallas_call x1, Pallas kernels: 13.8 us -> 11.4 us  [per_device(): pl.pallas_call(upward_kernel, out_shape=[shaped(512, 128), shaped(64, 128...]
  transfers between devices with their start and end apart: 4 -> 4, of which waited for: 4 -> 1; matrix products, arithmetic and copies ran while one was open for 1% -> 1% of each run, Pallas kernels for 0% -> 14%
where the time goes in v2:
time: 86.7 us; the launch traced here: 86.4 us
  Pallas kernels  69.4 us (80%)
  starting transfers between devices  13.4 us (15%)
  other arithmetic  1.9 us (2%)
    pallas_call x1, Pallas kernels, per_device(): pl.pallas_call(downward_kernel, out_shape=shaped(64, 256), in_specs=vmem(...  46.4 us
    ppermute x4, starting transfers between devices, neighbours(): return (lax.ppermute(high, axis, up), lax.ppermute(low, axis, down))  13.4 us
    pallas_call x1, Pallas kernels, per_device(): pl.pallas_call(upward_kernel, out_shape=[shaped(512, 128), shaped(64, 128...  11.4 us
    pallas_call x1, Pallas kernels, per_device(): pl.pallas_call(near_x_kernel, out_shape=shaped(128, 128), in_specs=vmem(6...  7.2 us
    pallas_call x1, Pallas kernels, per_device(): pl.pallas_call(near_own_kernel, out_shape=shaped(128, 128), in_specs=vmem...  4.49 us
  transfers between devices with their start and end apart: 4, of which 1 were waited for; matrix products, arithmetic and copies ran while one was open for 1% of the time, Pallas kernels for 14%

profile of v2, /device:TPU:41, one launch (start us, length us, event | category | flops | bytes accessed | tf_op | source)
XLA Modules:
  0.0 86.4 jit_solution(10316605065727496327)
XLA Ops:
  0.0 11.4 %upward.1 = (f32[512,128]{1,0:T(8,128)}, f32[64,128]{1,0:T(8,128)}, f32[8,128]{1,0:T(8,128)}, f32[360,128]{1,0:T(8,128)}, f32[360,128]{1,0:T(8,128)}, /*index=5*...) custom-call(f32[3,64,256]{2,1,0:T(8,128)} %bitcast.4, f32[64,256]{1,0:T(8,128)} %bitcast.10, s32[64,8]{1,0:T(8,128)} %bitcast.8, ...), custom_call_target="tpu_custom_call" | custom-call | tf_op jit(solution)/shard_map/upward/pallas_call | solution.py:783
  11.4 4.1 %collective-permute-start = (f32[360,128]{1,0:T(8,128)}, f32[360,128]{1,0:T(8,128)S(1)}, u32[]{:S(2)}, u32[]{:S(2)}) collective-permute-start(f32[360,128]{1,0:T(8,128)} %get-tuple-element.17), channel_id=1, source_target_pairs={{0,16},{16,32},{32,48},{48,64},{64,80},{80,96},{96,112},{1,17},{17... | collective-permute-start | bytes 552968 | tf_op jit(solution)/shard_map/ppermute | solution.py:775
  15.5 1.9 %collective-permute-start.1 = (f32[360,128]{1,0:T(8,128)}, f32[360,128]{1,0:T(8,128)S(1)}, u32[]{:S(2)}, u32[]{:S(2)}) collective-permute-start(f32[360,128]{1,0:T(8,128)} %get-tuple-element.18), channel_id=1, source_target_pairs={{16,0},{32,16},{48,32},{64,48},{80,64},{96,80},{112,96},{17,1},{33... | collective-permute-start | bytes 552968 | tf_op jit(solution)/shard_map/ppermute | solution.py:775
  17.4 4.5 %near_own.1.before = f32[128,128]{1,0:T(8,128)} custom-call(f32[3,64,256]{2,1,0:T(8,128)} %bitcast.5, f32[64,256]{1,0:T(8,128)} %get-tuple-element.16.weighted, bf16[256,1152]{1,0:T(8,128)(2,1)} %constant.28.clone.pick.near_pick), custom_call_target="tpu_custom_call" | custom-call | flops 10000000 | bytes 10000000 | tf_op jit(solution)/shard_map/near_own/pallas_call | solution.py:817
  21.9 0.0 collective-permute-done.x_low
  21.9 0.0 copy-start
  21.9 0.6 collective-permute-done.1.x_high
  22.6 0.0 copy-start.1
  22.6 1.0 %pad_maximum_fusion = f32[360,128]{1,0:T(8,128)S(1)} fusion(f32[64,128]{1,0:T(8,128)S(1)} %get-tuple-element.31, f32[64,128]{1,0:T(8,128)S(1)} %get-tuple-element.28, f32[232,128]{1,0:T(8,128)} %get-tuple-element.25), kind=kLoop, calls=%fused_computation | loop fusion | flops 92160 | bytes 368640 | tf_op jit(solution)/shard_map/concatenate | solution.py:831
  23.6 3.1 %collective-permute-start.2 = (f32[360,128]{1,0:T(8,128)S(1)}, f32[360,128]{1,0:T(8,128)S(1)}, u32[]{:S(2)}, u32[]{:S(2)}) collective-permute-start(f32[360,128]{1,0:T(8,128)S(1)} %pad_maximum_fusion), channel_id=1, source_target_pairs={{0,1},{1,2},{2,3},{3,4},{4,5},{5,6},{6,7},{7,8},{8,9},{9,10},{10,1... | collective-permute-start | bytes 552968 | tf_op jit(solution)/shard_map/ppermute | solution.py:775
  26.7 0.9 %pad_maximum_fusion.1 = f32[360,128]{1,0:T(8,128)S(1)} fusion(f32[64,128]{1,0:T(8,128)S(1)} %get-tuple-element.32, f32[64,128]{1,0:T(8,128)S(1)} %get-tuple-element.27, f32[232,128]{1,0:T(8,128)} %get-tuple-element.26), kind=kLoop, calls=%fused_computation.1 | loop fusion | flops 92160 | bytes 368640 | tf_op jit(solution)/shard_map/concatenate | solution.py:830
  27.6 4.3 %collective-permute-start.3 = (f32[360,128]{1,0:T(8,128)S(1)}, f32[360,128]{1,0:T(8,128)S(1)}, u32[]{:S(2)}, u32[]{:S(2)}) collective-permute-start(f32[360,128]{1,0:T(8,128)S(1)} %pad_maximum_fusion.1), channel_id=1, source_target_pairs={{1,0},{2,1},{3,2},{4,3},{5,4},{6,5},{7,6},{8,7},{9,8},{10,9},{11,1... | collective-permute-start | bytes 552968 | tf_op jit(solution)/shard_map/ppermute | solution.py:775
  31.9 0.0 copy-done
  31.9 0.0 copy-done.1
  31.9 7.2 %near_x.1.before = f32[128,128]{1,0:T(8,128)} custom-call(f32[3,64,256]{2,1,0:T(8,128)} %bitcast.6, f32[64,256]{1,0:T(8,128)} %get-tuple-element.16.weighted, f32[360,128]{1,0:T(8,128)} %copy-done, f32[360,128]{1,0:T(8,128)} %copy-done.1, bf16[256,1152]{1,0:T(8,128)(2,1)} %constant.28.clone.pick.near_pick, f32[128,128]{1,0:T(8,128)} %near_own.1.before), custom_call_target="tpu_custom_call" | custom-call | flops 20000000 | bytes 20000000 | tf_op jit(solution)/shard_map/near_x/pallas_call | solution.py:834
  39.1 0.0 collective-permute-done.2.y_low
  39.1 0.0 copy-start.2
  39.1 0.0 collective-permute-done.3.y_high
  39.1 0.0 copy-start.3
  39.1 0.6 copy-done.2
  39.8 0.1 copy-done.3
  39.8 46.4 %downward.1 = f32[64,256]{1,0:T(8,128)} custom-call(f32[3,64,256]{2,1,0:T(8,128)} %bitcast.7, f32[64,256]{1,0:T(8,128)} %get-tuple-element.16.weighted, s32[64,8]{1,0:T(8,128)} %bitcast.9, f32[128,128]{1,0:T(8,128)} %near_x.1.before, f32[512,128]{1,0:T(8,128)} %get-tuple-element.22.leaf, f32[64,128]{1,0:T(8,128)} %get-tuple-element.23.par, ...), custom_call_target="tpu_custom_call" | custom-call | tf_op jit(solution)/shard_map/downward/pallas_call | solution.py:844
  (1 shorter events, 0.0 us)
Async XLA Ops:
  11.4 10.5 %collective-permute-start = (f32[360,128]{1,0:T(8,128)}, f32[360,128]{1,0:T(8,128)S(1)}, u32[]{:S(2)}, u32[]{:S(2)}) collective-permute-start(f32[360,128]{1,0:T(8,128)} %get-tuple-element.17), channel_id=1, source_target_pairs={{0,16},{16,32},{32,48},{48,64},{64,80},{80,96},{96,112},{1,17},{17... | collective-permute-start | bytes 552968 | tf_op jit(solution)/shard_map/ppermute | solution.py:775
  15.5 7.1 %collective-permute-start.1 = (f32[360,128]{1,0:T(8,128)}, f32[360,128]{1,0:T(8,128)S(1)}, u32[]{:S(2)}, u32[]{:S(2)}) collective-permute-start(f32[360,128]{1,0:T(8,128)} %get-tuple-element.18), channel_id=1, source_target_pairs={{16,0},{32,16},{48,32},{64,48},{80,64},{96,80},{112,96},{17,1},{33... | collective-permute-start | bytes 552968 | tf_op jit(solution)/shard_map/ppermute | solution.py:775
  21.9 10.0 %copy-start = (f32[360,128]{1,0:T(8,128)}, f32[360,128]{1,0:T(8,128)S(1)}, u32[]{:S(2)}) copy-start(f32[360,128]{1,0:T(8,128)S(1)} %collective-permute-done.x_low) | copy-start | bytes 552964
  22.6 9.3 %copy-start.1 = (f32[360,128]{1,0:T(8,128)}, f32[360,128]{1,0:T(8,128)S(1)}, u32[]{:S(2)}) copy-start(f32[360,128]{1,0:T(8,128)S(1)} %collective-permute-done.1.x_high) | copy-start | bytes 552964
  23.6 15.5 %collective-permute-start.2 = (f32[360,128]{1,0:T(8,128)S(1)}, f32[360,128]{1,0:T(8,128)S(1)}, u32[]{:S(2)}, u32[]{:S(2)}) collective-permute-start(f32[360,128]{1,0:T(8,128)S(1)} %pad_maximum_fusion), channel_id=1, source_target_pairs={{0,1},{1,2},{2,3},{3,4},{4,5},{5,6},{6,7},{7,8},{8,9},{9,10},{10,1... | collective-permute-start | bytes 552968 | tf_op jit(solution)/shard_map/ppermute | solution.py:775
  27.6 11.5 %collective-permute-start.3 = (f32[360,128]{1,0:T(8,128)S(1)}, f32[360,128]{1,0:T(8,128)S(1)}, u32[]{:S(2)}, u32[]{:S(2)}) collective-permute-start(f32[360,128]{1,0:T(8,128)S(1)} %pad_maximum_fusion.1), channel_id=1, source_target_pairs={{1,0},{2,1},{3,2},{4,3},{5,4},{6,5},{7,6},{8,7},{9,8},{10,9},{11,1... | collective-permute-start | bytes 552968 | tf_op jit(solution)/shard_map/ppermute | solution.py:775
  39.1 0.7 copy-start.2
  39.1 0.7 copy-start.3

commit v3 on v2

--- a/solution.py
+++ b/solution.py
@@ -18,6 +18,9 @@
 PACKED = FACE + 2 * CORNER
 FACE_PAR, FACE_GRAND, FACE_NEAR = 128, 160, 168
 COR_PAR, COR_GRAND, COR_NEAR = 32, 48, 56
+
+
+SIDEWAYS = (0, 2, 3, 5, 6, 8)
 
 
 def node_cos():
@@ -80,7 +83,7 @@
         for ln in range(128):
             row = near_row[int(lane_x[ln]) + dx, int(lane_y[ln]) + dy]
             near_pick[lane_z[ln] * 128 + row, k, ln] = 1
-    near_pick = near_pick.reshape(256, 1152)
+    near_pick = near_pick[:, SIDEWAYS + (1, 7, 4)].reshape(256, 1152)
 
     leaf_row = {}
     for x in range(8):
@@ -295,36 +298,43 @@
                 return tuple(result)
 
             zero = jnp.zeros((8, 128), F32)
-            sums = lax.fori_loop(0, 32, slot, (zero,) * 32, unroll=4)
+            sums = lax.fori_loop(0, 32, slot, (zero,) * 32, unroll=8)
             for n in range(32):
                 moments[c, (half * 32 + n) * 8 : (half * 32 + n) * 8 + 8, :] = sums[n]
         return carry
 
     lax.fori_loop(0, 4, chunk, 0)
     compress_t = split2(compress[...].T)
-    for c in range(4):
-        small = mm3(compress_t, split2(moments[c])).T
-        for z in range(2):
-            leaf[pl.ds(c + 4 * z, 64, stride=8), :] = small[z * 64 : z * 64 + 64, :]
+    for first in (0, 2):
+        pair = jnp.concatenate([moments[first], moments[first + 1]], axis=1)
+        small = mm3(compress_t, split2(pair)).T
+        for c in (first, first + 1):
+            for z in range(2):
+                top = (c - first) * 128 + z * 64
+                leaf[pl.ds(c + 4 * z, 64, stride=8), :] = small[top : top + 64, :]
 
     step = split2(up_z[...])
-
-    def join_z(low, high, target):
-        for block in range(4):
-            rows = slice(block * 128, block * 128 + 128)
-            pair = jnp.concatenate([low[rows, :], high[rows, :]], axis=0)
-            target[rows, :] = mm3(step, split2(pair))
-
-    rough = []
+    for block in range(4):
+        rows = slice(block * 128, block * 128 + 128)
+        pair = jnp.concatenate(
+            [
+                jnp.concatenate([moments[cz, rows, :], moments[2 + cz, rows, :]], axis=1)
+                for cz in range(2)
+            ],
+            axis=0,
+        )
+        joined = mm3(step, split2(pair))
+        for q in range(2):
+            parents[q, rows, :] = joined[:, 128 * q : 128 * q + 128]
     for q in range(2):
-        join_z(moments.at[2 * q], moments.at[2 * q + 1], work_a)
-        mix_x(work_a, work_b, lanes, 0, True)
+        mix_x(parents.at[q], work_b, lanes, 0, True)
         mix_y(work_b, parents.at[q], lanes, 1, True)
-        rough.append(mm3(compress_t, split2(parents[q])).T)
-    par[...] = jnp.dot(
-        pick_par[...], jnp.concatenate(rough, axis=0), precision=EXACT, preferred_element_type=F32
-    )
-    join_z(parents.at[0], parents.at[1], work_a)
+    rough = mm3(compress_t, split2(jnp.concatenate([parents[0], parents[1]], axis=1))).T
+    par[...] = jnp.dot(pick_par[...], rough, precision=EXACT, preferred_element_type=F32)
+    for block in range(4):
+        rows = slice(block * 128, block * 128 + 128)
+        pair = jnp.concatenate([parents[0, rows, :], parents[1, rows, :]], axis=0)
+        work_a[rows, :] = mm3(step, split2(pair))
     mix_x(work_a, work_b, lanes, 2, True)
     mix_y(work_b, work_a, lanes, 3, True)
     rough = mm3(compress_t, split2(work_a[...])).T
@@ -393,27 +403,30 @@
                     columns[row, target : target + 1, :] = buffer[source : source + 1, :]
 
 
-def stage_sources(columns, pick, shifts, sources, squares):
+def stage_sources(columns, pick, column, shifts, sources, squares):
     empty = jnp.zeros((32, 128), F32)
     for component in range(4):
         low = columns[2 * component].T
         high = columns[2 * component + 1].T
         left = jnp.concatenate([empty, low, high[0:32, :]], axis=0)
         right = jnp.concatenate([low[96:128, :], high, empty], axis=0)
-        pieces = split3(jnp.concatenate([left, right], axis=1))
-        for n, k in enumerate(shifts):
-            table = pick[:, k * 128 : k * 128 + 128]
-            value = (mm(pieces[0], table) + mm(pieces[1], table)) + mm(pieces[2], table)
-            if component == 3:
-                sources[3, n] = value
-                continue
-            offset = (k // 3 - 1, k % 3 - 1, 0)[component] - 0.5
-            value = value + offset
-            sources[component, n] = -2.0 * value
-            if component == 0:
-                squares[n] = value * value + SOFTENING
-            else:
-                squares[n] = squares[n] + value * value
+        pieces = jnp.concatenate(split3(jnp.concatenate([left, right], axis=1)), axis=0)
+        for first in range(0, len(shifts), 2):
+            width = 128 * min(2, len(shifts) - first)
+            chosen = mm(pieces, pick[:, column + 128 * first : column + 128 * first + width])
+            chosen = (chosen[0:192] + chosen[192:384]) + chosen[384:576]
+            for n in range(first, first + width // 128):
+                value = chosen[:, 128 * (n - first) : 128 * (n - first) + 128]
+                if component == 3:
+                    sources[3, n] = value
+                    continue
+                offset = (shifts[n] // 3 - 1, shifts[n] % 3 - 1, 0)[component] - 0.5
+                value = value + offset
+                sources[component, n] = -2.0 * value
+                if component == 0:
+                    squares[n] = value * value + SOFTENING
+                else:
+                    squares[n] = squares[n] + value * value
 
 
 def pair_steps(targets, start, dz, sources, squares, n, base, count, own, sums):
@@ -449,7 +462,7 @@
 
 def near_part(shifts, pos, weighted, x_faces, pick, near, before, columns, sources, squares, targets):
     stage_columns(columns, pos, weighted, x_faces, ())
-    stage_sources(columns, pick, shifts, sources, squares)
+    stage_sources(columns, pick, 1024 if shifts == (4,) else 768, shifts, sources, squares)
     for component in range(3):
         targets[component] = lanes_first(pos[component]) - 0.5
 
@@ -485,9 +498,6 @@
     )
 
 
-SIDEWAYS = (0, 2, 3, 5, 6, 8)
-
-
 ROW_STARTS = (0, 49, 98, 138, 178, 218, 267, 316)
 
 
@@ -496,7 +506,7 @@
     expand, lanes, down_z, spread, near_pick, leaf_pick, small_pick, place_leaf, place_small,
     out,
     weights, staged, small, leaf_high, leaf_low, small_high, small_low, right_high, right_low,
-    sums, flat, basis_x, basis_y, basis_z, local, work_a, work_b, work_c, far,
+    sums, flat, basis_x, basis_y, basis_z, local, work_a, work_b, work_c, parents, far,
     near, columns, sources, squares, targets, arrivals,
 ):
     copies = [
@@ -512,7 +522,7 @@
 
     near[...] = before[...]
     stage_columns(columns, pos, weighted, (x_low, x_high), (y_low, y_high))
-    stage_sources(columns, near_pick, SIDEWAYS, sources, squares)
+    stage_sources(columns, near_pick, 0, SIDEWAYS, sources, squares)
     for component in range(3):
         flat[component] = lanes_first(pos[component])
         targets[component] = flat[component] - 0.5
@@ -673,13 +683,15 @@
             last = start + 42
         translate(dx, 3, xs, (0,), last, False, row, high)
 
-    grow = split2(expand[...].T)
+    grow, grow_low = split2(expand[...].T)
+    grow_both = jnp.concatenate([grow, grow_low], axis=1)
     pairs = [(px, py) for px in both for py in both]
 
-    def expanded(rows, place):
-        flipped = split2(rows.T)
-        placed = tuple(mm(piece, place).astype(BF16) for piece in flipped)
-        return mm3(grow, placed)
+    def expanded(parts):
+        placed = [[mm(piece, place).astype(BF16) for piece in split2(rows.T)] for rows, place in parts]
+        high = jnp.concatenate([p[0] for p in placed], axis=1)
+        low = jnp.concatenate([p[1] for p in placed], axis=1)
+        return mm(grow_both, jnp.concatenate([high, high], axis=0)) + mm(grow, low)
 
     pieces = []
     for q in range(2):
@@ -694,31 +706,32 @@
     coarse = jnp.concatenate(pieces, axis=0)
     step = split2(down_z[...])
 
-    work_a[...] = expanded(coarse, place_small[2])
+    def share(value, source, low, high):
+        for block in range(4):
+            rows = slice(block * 128, block * 128 + 128)
+            carried = mm3(step, split2(source[rows, :]))
+            low[rows, :] = value[rows, 0:128] + carried[0:128]
+            high[rows, :] = value[rows, 128:256] + carried[128:256]
+
+    work_a[...] = expanded([(coarse, place_small[2])])
     mix_x(work_a, work_b, lanes, 2, False)
     mix_y(work_b, work_c, lanes, 3, False)
-
+    share(
+        expanded([(coarse, place_small[0]), (coarse, place_small[1])]),
+        work_c, parents.at[0], parents.at[1],
+    )
     for q in range(2):
-        side = tuple(piece[q * 128 : q * 128 + 128, :] for piece in step)
-        work_a[...] = expanded(coarse, place_small[q])
-        for block in range(4):
-            rows = slice(block * 128, block * 128 + 128)
-            work_a[rows, :] = work_a[rows, :] + mm3(side, split2(work_c[rows, :]))
-        mix_x(work_a, work_b, lanes, 0, False)
+        mix_x(parents.at[q], work_b, lanes, 0, False)
         mix_y(work_b, work_a, lanes, 1, False)
+        parts = []
         for cz in range(2):
             rows = [
                 sums[px * 2 + py, (q + 2 * z) * 16 : (q + 2 * z) * 16 + 16, cz * 128 : cz * 128 + 128]
                 for z in range(2)
                 for px, py in pairs
             ]
-            side = tuple(piece[cz * 128 : cz * 128 + 128, :] for piece in step)
-            local[2 * q + cz] = expanded(jnp.concatenate(rows, axis=0), place_leaf[...])
-            for block in range(4):
-                part = slice(block * 128, block * 128 + 128)
-                local[2 * q + cz, part, :] = local[2 * q + cz, part, :] + mm3(
-                    side, split2(work_a[part, :])
-                )
+            parts.append((jnp.concatenate(rows, axis=0), place_leaf[...]))
+        share(expanded(parts), work_a, local.at[2 * q], local.at[2 * q + 1])
 
     def chunk(c, carry):
         start = pl.multiple_of(c * 32, 32)
@@ -865,6 +878,7 @@
             pltpu.VMEM((512, 128), F32),
             pltpu.VMEM((512, 128), F32),
             pltpu.VMEM((512, 128), F32),
+            pltpu.VMEM((2, 512, 128), F32),
             pltpu.VMEM((128, 128), F32),
             pltpu.VMEM((128, 128), F32),
             *near_scratch(6),

time: 86.7 us -> 84 us (0.969)
  Pallas kernels: 69.4 us -> 66.6 us
    pallas_call x1, Pallas kernels: 46.4 us -> 44.9 us  [per_device(): pl.pallas_call(downward_kernel, out_shape=shaped(64, 256), in_specs=vmem(...]
    pallas_call x1, Pallas kernels: 11.4 us -> 10.5 us  [per_device(): pl.pallas_call(upward_kernel, out_shape=[shaped(512, 128), shaped(64, 128...]
  transfers between devices with their start and end apart: 4 -> 4, of which waited for: 1 -> 1; matrix products, arithmetic and copies ran while one was open for 1% -> 1% of each run, Pallas kernels for 14% -> 13%
where the time goes in v3:
time: 84 us; the launch traced here: 83.7 us
  Pallas kernels  66.6 us (79%)
  starting transfers between devices  13.6 us (16%)
  other arithmetic  1.9 us (2%)
    pallas_call x1, Pallas kernels, per_device(): pl.pallas_call(downward_kernel, out_shape=shaped(64, 256), in_specs=vmem(...  44.9 us
    ppermute x4, starting transfers between devices, neighbours(): return (lax.ppermute(high, axis, up), lax.ppermute(low, axis, down))  13.6 us
    pallas_call x1, Pallas kernels, per_device(): pl.pallas_call(upward_kernel, out_shape=[shaped(512, 128), shaped(64, 128...  10.5 us
    pallas_call x1, Pallas kernels, per_device(): pl.pallas_call(near_x_kernel, out_shape=shaped(128, 128), in_specs=vmem(6...  6.71 us
    pallas_call x1, Pallas kernels, per_device(): pl.pallas_call(near_own_kernel, out_shape=shaped(128, 128), in_specs=vmem...  4.49 us
  transfers between devices with their start and end apart: 4, of which 1 were waited for; matrix products, arithmetic and copies ran while one was open for 1% of the time, Pallas kernels for 13%

profile of v3, /device:TPU:41, one launch (start us, length us, event | category | flops | bytes accessed | tf_op | source)
XLA Modules:
  0.0 83.7 jit_solution(7669993437778392146)
XLA Ops:
  0.0 10.5 %upward.1 = (f32[512,128]{1,0:T(8,128)}, f32[64,128]{1,0:T(8,128)}, f32[8,128]{1,0:T(8,128)}, f32[360,128]{1,0:T(8,128)}, f32[360,128]{1,0:T(8,128)}, /*index=5*...) custom-call(f32[3,64,256]{2,1,0:T(8,128)} %bitcast.4, f32[64,256]{1,0:T(8,128)} %bitcast.10, s32[64,8]{1,0:T(8,128)} %bitcast.8, ...), custom_call_target="tpu_custom_call" | custom-call | tf_op jit(solution)/shard_map/upward/pallas_call | solution.py:796
  10.5 4.1 %collective-permute-start = (f32[360,128]{1,0:T(8,128)}, f32[360,128]{1,0:T(8,128)S(1)}, u32[]{:S(2)}, u32[]{:S(2)}) collective-permute-start(f32[360,128]{1,0:T(8,128)} %get-tuple-element.17), channel_id=1, source_target_pairs={{0,16},{16,32},{32,48},{48,64},{64,80},{80,96},{96,112},{1,17},{17... | collective-permute-start | bytes 552968 | tf_op jit(solution)/shard_map/ppermute | solution.py:788
  14.6 1.9 %collective-permute-start.1 = (f32[360,128]{1,0:T(8,128)}, f32[360,128]{1,0:T(8,128)S(1)}, u32[]{:S(2)}, u32[]{:S(2)}) collective-permute-start(f32[360,128]{1,0:T(8,128)} %get-tuple-element.18), channel_id=1, source_target_pairs={{16,0},{32,16},{48,32},{64,48},{80,64},{96,80},{112,96},{17,1},{33... | collective-permute-start | bytes 552968 | tf_op jit(solution)/shard_map/ppermute | solution.py:788
  16.5 4.5 %near_own.1.before = f32[128,128]{1,0:T(8,128)} custom-call(f32[3,64,256]{2,1,0:T(8,128)} %bitcast.5, f32[64,256]{1,0:T(8,128)} %get-tuple-element.16.weighted, bf16[256,1152]{1,0:T(8,128)(2,1)} %constant.28.clone.pick.near_pick), custom_call_target="tpu_custom_call" | custom-call | flops 10000000 | bytes 10000000 | tf_op jit(solution)/shard_map/near_own/pallas_call | solution.py:830
  21.0 0.0 collective-permute-done.x_low
  21.0 0.0 copy-start
  21.0 0.6 collective-permute-done.1.x_high
  21.7 0.0 copy-start.1
  21.7 1.0 %pad_maximum_fusion = f32[360,128]{1,0:T(8,128)S(1)} fusion(f32[64,128]{1,0:T(8,128)S(1)} %get-tuple-element.31, f32[64,128]{1,0:T(8,128)S(1)} %get-tuple-element.28, f32[232,128]{1,0:T(8,128)} %get-tuple-element.25), kind=kLoop, calls=%fused_computation | loop fusion | flops 92160 | bytes 368640 | tf_op jit(solution)/shard_map/concatenate | solution.py:844
  22.7 3.1 %collective-permute-start.2 = (f32[360,128]{1,0:T(8,128)S(1)}, f32[360,128]{1,0:T(8,128)S(1)}, u32[]{:S(2)}, u32[]{:S(2)}) collective-permute-start(f32[360,128]{1,0:T(8,128)S(1)} %pad_maximum_fusion), channel_id=1, source_target_pairs={{0,1},{1,2},{2,3},{3,4},{4,5},{5,6},{6,7},{7,8},{8,9},{9,10},{10,1... | collective-permute-start | bytes 552968 | tf_op jit(solution)/shard_map/ppermute | solution.py:788
  25.8 0.9 %pad_maximum_fusion.1 = f32[360,128]{1,0:T(8,128)S(1)} fusion(f32[64,128]{1,0:T(8,128)S(1)} %get-tuple-element.32, f32[64,128]{1,0:T(8,128)S(1)} %get-tuple-element.27, f32[232,128]{1,0:T(8,128)} %get-tuple-element.26), kind=kLoop, calls=%fused_computation.1 | loop fusion | flops 92160 | bytes 368640 | tf_op jit(solution)/shard_map/concatenate | solution.py:843
  26.7 4.5 %collective-permute-start.3 = (f32[360,128]{1,0:T(8,128)S(1)}, f32[360,128]{1,0:T(8,128)S(1)}, u32[]{:S(2)}, u32[]{:S(2)}) collective-permute-start(f32[360,128]{1,0:T(8,128)S(1)} %pad_maximum_fusion.1), channel_id=1, source_target_pairs={{1,0},{2,1},{3,2},{4,3},{5,4},{6,5},{7,6},{8,7},{9,8},{10,9},{11,1... | collective-permute-start | bytes 552968 | tf_op jit(solution)/shard_map/ppermute | solution.py:788
  31.2 0.0 copy-done
  31.2 0.0 copy-done.1
  31.2 6.7 %near_x.1.before = f32[128,128]{1,0:T(8,128)} custom-call(f32[3,64,256]{2,1,0:T(8,128)} %bitcast.6, f32[64,256]{1,0:T(8,128)} %get-tuple-element.16.weighted, f32[360,128]{1,0:T(8,128)} %copy-done, f32[360,128]{1,0:T(8,128)} %copy-done.1, bf16[256,1152]{1,0:T(8,128)(2,1)} %constant.28.clone.pick.near_pick, f32[128,128]{1,0:T(8,128)} %near_own.1.before), custom_call_target="tpu_custom_call" | custom-call | flops 20000000 | bytes 20000000 | tf_op jit(solution)/shard_map/near_x/pallas_call | solution.py:847
  37.9 0.0 collective-permute-done.2.y_low
  37.9 0.0 copy-start.2
  37.9 0.0 collective-permute-done.3.y_high
  37.9 0.0 copy-start.3
  37.9 0.6 copy-done.2
  38.6 0.1 copy-done.3
  38.6 44.9 %downward.1 = f32[64,256]{1,0:T(8,128)} custom-call(f32[3,64,256]{2,1,0:T(8,128)} %bitcast.7, f32[64,256]{1,0:T(8,128)} %get-tuple-element.16.weighted, s32[64,8]{1,0:T(8,128)} %bitcast.9, f32[128,128]{1,0:T(8,128)} %near_x.1.before, f32[512,128]{1,0:T(8,128)} %get-tuple-element.22.leaf, f32[64,128]{1,0:T(8,128)} %get-tuple-element.23.par, ...), custom_call_target="tpu_custom_call" | custom-call | tf_op jit(solution)/shard_map/downward/pallas_call | solution.py:857
  (1 shorter events, 0.0 us)
Async XLA Ops:
  10.5 10.5 %collective-permute-start = (f32[360,128]{1,0:T(8,128)}, f32[360,128]{1,0:T(8,128)S(1)}, u32[]{:S(2)}, u32[]{:S(2)}) collective-permute-start(f32[360,128]{1,0:T(8,128)} %get-tuple-element.17), channel_id=1, source_target_pairs={{0,16},{16,32},{32,48},{48,64},{64,80},{80,96},{96,112},{1,17},{17... | collective-permute-start | bytes 552968 | tf_op jit(solution)/shard_map/ppermute | solution.py:788
  14.6 7.1 %collective-permute-start.1 = (f32[360,128]{1,0:T(8,128)}, f32[360,128]{1,0:T(8,128)S(1)}, u32[]{:S(2)}, u32[]{:S(2)}) collective-permute-start(f32[360,128]{1,0:T(8,128)} %get-tuple-element.18), channel_id=1, source_target_pairs={{16,0},{32,16},{48,32},{64,48},{80,64},{96,80},{112,96},{17,1},{33... | collective-permute-start | bytes 552968 | tf_op jit(solution)/shard_map/ppermute | solution.py:788
  21.0 10.1 %copy-start = (f32[360,128]{1,0:T(8,128)}, f32[360,128]{1,0:T(8,128)S(1)}, u32[]{:S(2)}) copy-start(f32[360,128]{1,0:T(8,128)S(1)} %collective-permute-done.x_low) | copy-start | bytes 552964
  21.7 9.5 %copy-start.1 = (f32[360,128]{1,0:T(8,128)}, f32[360,128]{1,0:T(8,128)S(1)}, u32[]{:S(2)}) copy-start(f32[360,128]{1,0:T(8,128)S(1)} %collective-permute-done.1.x_high) | copy-start | bytes 552964
  22.7 15.2 %collective-permute-start.2 = (f32[360,128]{1,0:T(8,128)S(1)}, f32[360,128]{1,0:T(8,128)S(1)}, u32[]{:S(2)}, u32[]{:S(2)}) collective-permute-start(f32[360,128]{1,0:T(8,128)S(1)} %pad_maximum_fusion), channel_id=1, source_target_pairs={{0,1},{1,2},{2,3},{3,4},{4,5},{5,6},{6,7},{7,8},{8,9},{9,10},{10,1... | collective-permute-start | bytes 552968 | tf_op jit(solution)/shard_map/ppermute | solution.py:788
  26.7 11.2 %collective-permute-start.3 = (f32[360,128]{1,0:T(8,128)S(1)}, f32[360,128]{1,0:T(8,128)S(1)}, u32[]{:S(2)}, u32[]{:S(2)}) collective-permute-start(f32[360,128]{1,0:T(8,128)S(1)} %pad_maximum_fusion.1), channel_id=1, source_target_pairs={{1,0},{2,1},{3,2},{4,3},{5,4},{6,5},{7,6},{8,7},{9,8},{10,9},{11,1... | collective-permute-start | bytes 552968 | tf_op jit(solution)/shard_map/ppermute | solution.py:788
  37.9 0.7 copy-start.2
  37.9 0.7 copy-start.3

commit v4 on v3

--- a/solution.py
+++ b/solution.py
@@ -167,7 +167,9 @@
         pick_par=np.asarray(pick_par, np.float32),
         pick_grand=np.asarray(pick_grand, np.float32),
         spread=half(spread),
-        near_pick=half(near_pick),
+        pick_side=half(near_pick[:, :768]),
+        pick_x=half(near_pick[:, 768:1024]),
+        pick_own=half(near_pick[:, 1024:]),
         leaf_pick=half(leaf_pick),
         small_pick=half(small_pick),
         place_leaf=half(place_leaf),
@@ -298,7 +300,7 @@
                 return tuple(result)
 
             zero = jnp.zeros((8, 128), F32)
-            sums = lax.fori_loop(0, 32, slot, (zero,) * 32, unroll=8)
+            sums = lax.fori_loop(0, 32, slot, (zero,) * 32, unroll=16)
             for n in range(32):
                 moments[c, (half * 32 + n) * 8 : (half * 32 + n) * 8 + 8, :] = sums[n]
         return carry
@@ -403,7 +405,7 @@
                     columns[row, target : target + 1, :] = buffer[source : source + 1, :]
 
 
-def stage_sources(columns, pick, column, shifts, sources, squares):
+def stage_sources(columns, pick, shifts, sources, squares):
     empty = jnp.zeros((32, 128), F32)
     for component in range(4):
         low = columns[2 * component].T
@@ -413,7 +415,7 @@
         pieces = jnp.concatenate(split3(jnp.concatenate([left, right], axis=1)), axis=0)
         for first in range(0, len(shifts), 2):
             width = 128 * min(2, len(shifts) - first)
-            chosen = mm(pieces, pick[:, column + 128 * first : column + 128 * first + width])
+            chosen = mm(pieces, pick[:, 128 * first : 128 * first + width])
             chosen = (chosen[0:192] + chosen[192:384]) + chosen[384:576]
             for n in range(first, first + width // 128):
                 value = chosen[:, 128 * (n - first) : 128 * (n - first) + 128]
@@ -462,7 +464,7 @@
 
 def near_part(shifts, pos, weighted, x_faces, pick, near, before, columns, sources, squares, targets):
     stage_columns(columns, pos, weighted, x_faces, ())
-    stage_sources(columns, pick, 1024 if shifts == (4,) else 768, shifts, sources, squares)
+    stage_sources(columns, pick, shifts, sources, squares)
     for component in range(3):
         targets[component] = lanes_first(pos[component]) - 0.5
 
@@ -522,7 +524,7 @@
 
     near[...] = before[...]
     stage_columns(columns, pos, weighted, (x_low, x_high), (y_low, y_high))
-    stage_sources(columns, near_pick, 0, SIDEWAYS, sources, squares)
+    stage_sources(columns, near_pick, SIDEWAYS, sources, squares)
     for component in range(3):
         flat[component] = lanes_first(pos[component])
         targets[component] = flat[component] - 0.5
@@ -764,7 +766,7 @@
                 )
             return carry
 
-        lax.fori_loop(0, 16, slots, 0, unroll=2)
+        lax.fori_loop(0, 16, slots, 0, unroll=4)
         return carry
 
     lax.fori_loop(0, 4, chunk, 0)
@@ -836,7 +838,7 @@
         compiler_params=limit,
         cost_estimate=pl.CostEstimate(flops=10**7, bytes_accessed=10**7, transcendentals=0),
         name="near_own",
-    )(pos, weighted, const["near_pick"])
+    )(pos, weighted, const["pick_own"])
     near_own, x_low, x_high = lax.optimization_barrier((near_own, x_low, x_high))
     first, second = slice(FACE, FACE + CORNER), slice(FACE + CORNER, PACKED)
     y_low, y_high = neighbours(
@@ -853,7 +855,7 @@
         compiler_params=limit,
         cost_estimate=pl.CostEstimate(flops=2 * 10**7, bytes_accessed=2 * 10**7, transcendentals=0),
         name="near_x",
-    )(pos, weighted, x_low, x_high, const["near_pick"], near_own)
+    )(pos, weighted, x_low, x_high, const["pick_x"], near_own)
     result = pl.pallas_call(
         downward_kernel,
         out_shape=shaped(64, 256),
@@ -888,7 +890,7 @@
         name="downward",
     )(
         pos, weighted, cells, near, leaf, par, grand, x_low, x_high, y_low, y_high, operators, expand,
-        const["lanes"], const["down_z"], const["spread"], const["near_pick"], const["leaf_pick"],
+        const["lanes"], const["down_z"], const["spread"], const["pick_side"], const["leaf_pick"],
         const["small_pick"], const["place_leaf"], const["place_small"],
     )
     return result.reshape(8, 8, 256)

time: 84 us -> 83.3 us (level)
  Pallas kernels: 66.6 us -> 65.6 us
where the time goes in v4:
time: 83.3 us; the launch traced here: 83 us
  Pallas kernels  65.6 us (79%)
  starting transfers between devices  13.6 us (16%)
  other arithmetic  1.9 us (2%)
  waiting for transfers between devices  0.89 us (1%)
    pallas_call x1, Pallas kernels, per_device(): pl.pallas_call(downward_kernel, out_shape=shaped(64, 256), in_specs=vmem(...  44.6 us
    ppermute x4, starting transfers between devices, neighbours(): return (lax.ppermute(high, axis, up), lax.ppermute(low, axis, down))  13.6 us
    pallas_call x1, Pallas kernels, per_device(): pl.pallas_call(upward_kernel, out_shape=[shaped(512, 128), shaped(64, 128...  10.3 us
    pallas_call x1, Pallas kernels, per_device(): pl.pallas_call(near_x_kernel, out_shape=shaped(128, 128), in_specs=vmem(6...  6.55 us
    pallas_call x1, Pallas kernels, per_device(): pl.pallas_call(near_own_kernel, out_shape=shaped(128, 128), in_specs=vmem...  4.26 us
  transfers between devices with their start and end apart: 4, of which 1 were waited for; matrix products, arithmetic and copies ran while one was open for 1% of the time, Pallas kernels for 13%

profile of v4, /device:TPU:41, one launch (start us, length us, event | category | flops | bytes accessed | tf_op | source)
XLA Modules:
  0.0 83.0 jit_solution(9977585617802408989)
XLA Ops:
  0.0 10.3 %upward.1 = (f32[512,128]{1,0:T(8,128)}, f32[64,128]{1,0:T(8,128)}, f32[8,128]{1,0:T(8,128)}, f32[360,128]{1,0:T(8,128)}, f32[360,128]{1,0:T(8,128)}, /*index=5*...) custom-call(f32[3,64,256]{2,1,0:T(8,128)} %bitcast.4, f32[64,256]{1,0:T(8,128)} %bitcast.10, s32[64,8]{1,0:T(8,128)} %bitcast.8, ...), custom_call_target="tpu_custom_call" | custom-call | tf_op jit(solution)/shard_map/upward/pallas_call | solution.py:798
  10.3 4.1 %collective-permute-start = (f32[360,128]{1,0:T(8,128)}, f32[360,128]{1,0:T(8,128)S(1)}, u32[]{:S(2)}, u32[]{:S(2)}) collective-permute-start(f32[360,128]{1,0:T(8,128)} %get-tuple-element.17), channel_id=1, source_target_pairs={{0,16},{16,32},{32,48},{48,64},{64,80},{80,96},{96,112},{1,17},{17... | collective-permute-start | bytes 552968 | tf_op jit(solution)/shard_map/ppermute | solution.py:790
  14.4 1.9 %collective-permute-start.1 = (f32[360,128]{1,0:T(8,128)}, f32[360,128]{1,0:T(8,128)S(1)}, u32[]{:S(2)}, u32[]{:S(2)}) collective-permute-start(f32[360,128]{1,0:T(8,128)} %get-tuple-element.18), channel_id=1, source_target_pairs={{16,0},{32,16},{48,32},{64,48},{80,64},{96,80},{112,96},{17,1},{33... | collective-permute-start | bytes 552968 | tf_op jit(solution)/shard_map/ppermute | solution.py:790
  16.3 4.3 %near_own.1.before = f32[128,128]{1,0:T(8,128)} custom-call(f32[3,64,256]{2,1,0:T(8,128)} %bitcast.5, f32[64,256]{1,0:T(8,128)} %get-tuple-element.16.weighted, bf16[256,128]{1,0:T(8,128)(2,1)} %constant.34.clone.pick), custom_call_target="tpu_custom_call" | custom-call | flops 10000000 | bytes 10000000 | tf_op jit(solution)/shard_map/near_own/pallas_call | solution.py:832
  20.6 0.0 collective-permute-done.x_low
  20.6 0.0 copy-start
  20.6 0.9 %collective-permute-done.1.x_high = f32[360,128]{1,0:T(8,128)S(1)} collective-permute-done((f32[360,128]{1,0:T(8,128)}, f32[360,128]{1,0:T(8,128)S(1)}, u32[]{:S(2)}, u32[]{:S(2)}) %collective-permute-start.1) | collective-permute-done | bytes 184352 | tf_op jit(solution)/shard_map/ppermute | solution.py:790
  21.5 0.0 copy-start.1
  21.5 1.0 %pad_maximum_fusion = f32[360,128]{1,0:T(8,128)S(1)} fusion(f32[64,128]{1,0:T(8,128)S(1)} %get-tuple-element.31, f32[64,128]{1,0:T(8,128)S(1)} %get-tuple-element.28, f32[232,128]{1,0:T(8,128)} %get-tuple-element.25), kind=kLoop, calls=%fused_computation | loop fusion | flops 92160 | bytes 368640 | tf_op jit(solution)/shard_map/concatenate | solution.py:846
  22.5 3.1 %collective-permute-start.2 = (f32[360,128]{1,0:T(8,128)S(1)}, f32[360,128]{1,0:T(8,128)S(1)}, u32[]{:S(2)}, u32[]{:S(2)}) collective-permute-start(f32[360,128]{1,0:T(8,128)S(1)} %pad_maximum_fusion), channel_id=1, source_target_pairs={{0,1},{1,2},{2,3},{3,4},{4,5},{5,6},{6,7},{7,8},{8,9},{9,10},{10,1... | collective-permute-start | bytes 552968 | tf_op jit(solution)/shard_map/ppermute | solution.py:790
  25.6 0.9 %pad_maximum_fusion.1 = f32[360,128]{1,0:T(8,128)S(1)} fusion(f32[64,128]{1,0:T(8,128)S(1)} %get-tuple-element.32, f32[64,128]{1,0:T(8,128)S(1)} %get-tuple-element.27, f32[232,128]{1,0:T(8,128)} %get-tuple-element.26), kind=kLoop, calls=%fused_computation.1 | loop fusion | flops 92160 | bytes 368640 | tf_op jit(solution)/shard_map/concatenate | solution.py:845
  26.5 4.5 %collective-permute-start.3 = (f32[360,128]{1,0:T(8,128)S(1)}, f32[360,128]{1,0:T(8,128)S(1)}, u32[]{:S(2)}, u32[]{:S(2)}) collective-permute-start(f32[360,128]{1,0:T(8,128)S(1)} %pad_maximum_fusion.1), channel_id=1, source_target_pairs={{1,0},{2,1},{3,2},{4,3},{5,4},{6,5},{7,6},{8,7},{9,8},{10,9},{11,1... | collective-permute-start | bytes 552968 | tf_op jit(solution)/shard_map/ppermute | solution.py:790
  31.0 0.0 copy-done
  31.0 0.0 copy-done.1
  31.0 6.5 %near_x.1.before = f32[128,128]{1,0:T(8,128)} custom-call(f32[3,64,256]{2,1,0:T(8,128)} %bitcast.6, f32[64,256]{1,0:T(8,128)} %get-tuple-element.16.weighted, f32[360,128]{1,0:T(8,128)} %copy-done, f32[360,128]{1,0:T(8,128)} %copy-done.1, bf16[256,256]{1,0:T(8,128)(2,1)} %constant.33.clone.pick, f32[128,128]{1,0:T(8,128)} %near_own.1.before), custom_call_target="tpu_custom_call" | custom-call | flops 20000000 | bytes 20000000 | tf_op jit(solution)/shard_map/near_x/pallas_call | solution.py:849
  37.5 0.0 collective-permute-done.2.y_low
  37.5 0.0 copy-start.2
  37.5 0.0 collective-permute-done.3.y_high
  37.6 0.0 copy-start.3
  37.6 0.6 copy-done.2
  38.2 0.1 copy-done.3
  38.3 44.6 %downward.1 = f32[64,256]{1,0:T(8,128)} custom-call(f32[3,64,256]{2,1,0:T(8,128)} %bitcast.7, f32[64,256]{1,0:T(8,128)} %get-tuple-element.16.weighted, s32[64,8]{1,0:T(8,128)} %bitcast.9, f32[128,128]{1,0:T(8,128)} %near_x.1.before, f32[512,128]{1,0:T(8,128)} %get-tuple-element.22.leaf, f32[64,128]{1,0:T(8,128)} %get-tuple-element.23.par, ...), custom_call_target="tpu_custom_call" | custom-call | tf_op jit(solution)/shard_map/downward/pallas_call | solution.py:859
  (1 shorter events, 0.0 us)
Async XLA Ops:
  10.3 10.3 %collective-permute-start = (f32[360,128]{1,0:T(8,128)}, f32[360,128]{1,0:T(8,128)S(1)}, u32[]{:S(2)}, u32[]{:S(2)}) collective-permute-start(f32[360,128]{1,0:T(8,128)} %get-tuple-element.17), channel_id=1, source_target_pairs={{0,16},{16,32},{32,48},{48,64},{64,80},{80,96},{96,112},{1,17},{17... | collective-permute-start | bytes 552968 | tf_op jit(solution)/shard_map/ppermute | solution.py:790
  14.4 7.1 %collective-permute-start.1 = (f32[360,128]{1,0:T(8,128)}, f32[360,128]{1,0:T(8,128)S(1)}, u32[]{:S(2)}, u32[]{:S(2)}) collective-permute-start(f32[360,128]{1,0:T(8,128)} %get-tuple-element.18), channel_id=1, source_target_pairs={{16,0},{32,16},{48,32},{64,48},{80,64},{96,80},{112,96},{17,1},{33... | collective-permute-start | bytes 552968 | tf_op jit(solution)/shard_map/ppermute | solution.py:790
  20.6 10.4 %copy-start = (f32[360,128]{1,0:T(8,128)}, f32[360,128]{1,0:T(8,128)S(1)}, u32[]{:S(2)}) copy-start(f32[360,128]{1,0:T(8,128)S(1)} %collective-permute-done.x_low) | copy-start | bytes 552964
  21.5 9.5 %copy-start.1 = (f32[360,128]{1,0:T(8,128)}, f32[360,128]{1,0:T(8,128)S(1)}, u32[]{:S(2)}) copy-start(f32[360,128]{1,0:T(8,128)S(1)} %collective-permute-done.1.x_high) | copy-start | bytes 552964
  22.5 15.1 %collective-permute-start.2 = (f32[360,128]{1,0:T(8,128)S(1)}, f32[360,128]{1,0:T(8,128)S(1)}, u32[]{:S(2)}, u32[]{:S(2)}) collective-permute-start(f32[360,128]{1,0:T(8,128)S(1)} %pad_maximum_fusion), channel_id=1, source_target_pairs={{0,1},{1,2},{2,3},{3,4},{4,5},{5,6},{6,7},{7,8},{8,9},{9,10},{10,1... | collective-permute-start | bytes 552968 | tf_op jit(solution)/shard_map/ppermute | solution.py:790
  26.5 11.0 %collective-permute-start.3 = (f32[360,128]{1,0:T(8,128)S(1)}, f32[360,128]{1,0:T(8,128)S(1)}, u32[]{:S(2)}, u32[]{:S(2)}) collective-permute-start(f32[360,128]{1,0:T(8,128)S(1)} %pad_maximum_fusion.1), channel_id=1, source_target_pairs={{1,0},{2,1},{3,2},{4,3},{5,4},{6,5},{7,6},{8,7},{9,8},{10,9},{11,1... | collective-permute-start | bytes 552968 | tf_op jit(solution)/shard_map/ppermute | solution.py:790
  37.5 0.7 copy-start.2
  37.6 0.7 copy-start.3
